TPU v7x, 512 devices: a whole 4x8x8 slice. The times are simulated.
512 devices in a mesh: grp: 32 (over y, x), row: 16 (over z, core).
Axes of the slice: x: 4, y: 8, z: 8, core: 2. Of those that a mesh axis runs over, the one named last changes fastest.
Arguments:
- activations: bfloat16 [262144, 4096], P(('grp', 'row')), may hold values from -2200 to 2200
- probe_matrix: bfloat16 [128, 4096], P(None, 'row'), may hold values from -0.09375 to 0.09375
Outputs:
- first_projected: float32 [128, 4096], P(None, ('grp', 'row'))
- projected: float32 [128, 4096], P(None, 'row')
All inputs are finite; a program needn't handle non-finite values.
Results may differ from a plain program's by a relative error of at most 0.0032.
Values may be sent and summed in bfloat16 or wider, within the bound.
A program may use at most 64 MiB of HBM per device.

v0:
```python
import jax
import jax.numpy as jnp
from jax import lax
from jax.sharding import PartitionSpec as P


def moments_local(sketch, activations):
    gram_term = lax.dot_general(
        sketch, sketch, (((1,), (1,)), ((), ())), preferred_element_type=jnp.float32
    )
    cross_term = jnp.dot(sketch, activations, preferred_element_type=jnp.float32)
    return (gram_term, cross_term)


def solve_lower(gram_term, cross_term):
    factor = jnp.linalg.cholesky(gram_term)
    return jax.scipy.linalg.solve_triangular(factor, cross_term, lower=True)


def reduce_final(summand):
    within = lax.psum_scatter(summand, "row", scatter_dimension=1, tiled=True)
    return lax.psum(within, "grp")


def own_columns(full_sum):
    share = full_sum.shape[1] // (lax.axis_size("grp") * lax.axis_size("row"))
    return lax.dynamic_slice_in_dim(full_sum, lax.axis_index(("grp", "row")) * share, share, 1)


def on_device(activations, probe_matrix):
    sketch = lax.dot_general(
        lax.all_gather(probe_matrix, "row", axis=1, tiled=True),
        activations,
        (((1,), (1,)), ((), ())),
        preferred_element_type=jnp.float32,
    ).astype(jnp.bfloat16)
    gram_local, cross_local = moments_local(sketch, activations)
    gram_total = lax.psum(gram_local, ("grp", "row"))
    solved = solve_lower(gram_total, cross_local)
    full_first = lax.psum(solved, ("grp", "row"))
    first_out = own_columns(full_first)
    back_proj = full_first.astype(jnp.bfloat16)
    sketch_next = lax.dot_general(
        back_proj, activations, (((1,), (1,)), ((), ())), preferred_element_type=jnp.float32
    ).astype(jnp.bfloat16)
    gram_next, cross_next = moments_local(sketch_next, activations)
    gram_second_total = lax.psum(gram_next, ("grp", "row"))
    return (first_out, reduce_final(solve_lower(gram_second_total, cross_next)))


def solution(mesh):
    return jax.shard_map(
        on_device,
        mesh=mesh,
        in_specs=(P(("grp", "row"), None), P(None, "row")),
        out_specs=(P(None, ("grp", "row")), P(None, "row")),
        check_vma=False,
    )
```

profile of v0, /device:TPU:14, one launch (start us, length us, event | category | flops | bytes accessed | tf_op | source)
XLA Modules:
  0.0 1123.6 jit_solution(16657917061821048715)
XLA Ops:
  7.2 0.0 all-gather.2.cloned.1.call-start
  7.2 0.7 all-gather.2.cloned.1.call-update
  7.9 0.0 all-reduce.5.cloned.1.call-start
  7.9 47.5 %all-gather.2.cloned.1.call-done = bf16[128,4096]{1,0:T(8,128)(2,1)} async-done(((bf16[128,256]{1,0:T(8,128)(2,1)}), bf16[128,4096]{1,0:T(8,128)(2,1)}) %all-gather.2.cloned.1.call-update) | async-done | bytes 1048592 | tf_op jit(solution)/shard_map/all_gather | solution.py:32
  55.4 4.0 convolution_convert_fusion.1
  59.5 0.8 fusion.9
  60.3 0.0 all-reduce.5.cloned.1.call-update
  60.3 0.0 all-reduce.7.cloned.1.call-start
  60.4 2.9 fusion.10
  63.3 255.3 %all-reduce.5.cloned.1.call-done = f32[128,128]{0,1:T(8,128)} async-done(((f32[128,128]{0,1:T(8,128)}), f32[128,128]{0,1:T(8,128)}) %all-reduce.5.cloned.1.call-update) | async-done | bytes 65552 | tf_op jit(solution)/shard_map/psum | solution.py:38
  318.5 0.9 copy.5
  319.5 0.9 fusion.8
  320.3 11.7 %cholesky.44 = f32[128,128]{1,0:T(8,128)S(1)} custom-call(f32[128,128]{1,0:T(8,128)S(1)} %fusion.8), custom_call_target="Cholesky" | custom-call | tf_op jit(solution)/shard_map/jit(cholesky)/cholesky | solution.py:16
  332.1 0.6 compare_reduce_fusion.1
  332.7 0.7 fusion.1
  333.4 9.8 custom-call.6
  343.2 3.2 fusion.6
  346.4 0.0 all-reduce.7.cloned.1.call-update
  346.5 0.0 all-reduce.9.cloned.1.call-start
  346.5 270.7 %all-reduce.7.cloned.1.call-done = f32[128,4096]{1,0:T(8,128)} async-done(((f32[128,4096]{1,0:T(8,128)}), f32[128,4096]{1,0:T(8,128)}) %all-reduce.7.cloned.1.call-update) | async-done | bytes 2097168 | tf_op jit(solution)/shard_map/psum | solution.py:40
  617.2 4.3 convolution_convert_fusion
  621.6 0.8 fusion.11
  622.4 0.0 all-reduce.9.cloned.1.call-update
  622.4 0.2 reduce-scatter.2.cloned.1.call-start
  622.7 2.9 fusion.12
  625.6 253.8 %all-reduce.9.cloned.1.call-done = f32[128,128]{0,1:T(8,128)} async-done(((f32[128,128]{0,1:T(8,128)}), f32[128,128]{0,1:T(8,128)}) %all-reduce.9.cloned.1.call-update) | async-done | bytes 65552 | tf_op jit(solution)/shard_map/psum | solution.py:47
  879.3 0.9 copy.7
  880.3 0.9 fusion.5
  881.1 11.7 %cholesky.55 = f32[128,128]{1,0:T(8,128)S(1)} custom-call(f32[128,128]{1,0:T(8,128)S(1)} %fusion.5), custom_call_target="Cholesky" | custom-call | tf_op jit(solution)/shard_map/jit(cholesky)/cholesky | solution.py:16
  892.9 0.6 compare_reduce_fusion
  893.5 0.7 fusion.2
  894.2 9.8 custom-call.7
  904.0 3.2 fusion.3
  907.2 0.0 reduce-scatter.2.cloned.1.call-update
  907.3 0.0 all-reduce.11.cloned.1.call-start
  907.3 54.9 %reduce-scatter.2.cloned.1.call-done = f32[128,256]{1,0:T(8,128)} async-done(((f32[128,4096]{1,0:T(8,128)}), f32[128,256]{1,0:T(8,128)}) %reduce-scatter.2.cloned.1.call-update) | async-done | bytes 131088 | tf_op jit(solution)/shard_map/reduce_scatter | solution.py:21
  962.2 0.0 all-reduce.11.cloned.1.call-update
  962.3 0.9 constant_dynamic-slice_fusion
  963.2 0.7 copy.8
  963.9 151.3 %all-reduce.11.cloned.1.call-done = f32[128,256]{1,0:T(8,128)} async-done(((f32[128,256]{1,0:T(8,128)}), f32[128,256]{1,0:T(8,128)}) %all-reduce.11.cloned.1.call-update) | async-done | bytes 131088 | tf_op jit(solution)/shard_map/psum | solution.py:22
  1115.2 1.6 copy.15
  (2 shorter events, 0.1 us)
Async XLA Ops:
  7.2 48.3 %all-gather.2.cloned.1.call-start = ((), (), s32[]{:S(2)}) async-start(), calls=%async_computation.1 | async-start | bytes 1114112 | tf_op jit(solution)/shard_map/all_gather | solution.py:32
  7.9 310.6 %all-reduce.5.cloned.1.call-start = ((), (), s32[]{:S(2)}) async-start(), calls=%async_computation.2 | async-start | bytes 131072 | tf_op jit(solution)/shard_map/psum | solution.py:38
  60.3 556.9 %all-reduce.7.cloned.1.call-start = ((), (), s32[]{:S(2)}) async-start(), calls=%async_computation.3 | async-start | bytes 4194304 | tf_op jit(solution)/shard_map/psum | solution.py:40
  346.5 532.9 %all-reduce.9.cloned.1.call-start = ((), (), s32[]{:S(2)}) async-start(), calls=%async_computation.4 | async-start | bytes 131072 | tf_op jit(solution)/shard_map/psum | solution.py:47
  622.4 339.8 %reduce-scatter.2.cloned.1.call-start = ((), (), s32[]{:S(2)}) async-start(), calls=%async_computation.5 | async-start | bytes 2228224 | tf_op jit(solution)/shard_map/reduce_scatter | solution.py:21
  907.3 207.9 %all-reduce.11.cloned.1.call-start = ((), (), s32[]{:S(2)}) async-start(), calls=%async_computation.6 | async-start | bytes 262144 | tf_op jit(solution)/shard_map/psum | solution.py:22
Sparse Core Ops, SparseCore 0:
  10.0 45.3 all-gather.1
  61.0 257.5 all-reduce.4
  346.6 270.6 all-reduce.6
  622.7 256.6 all-reduce.8
  907.4 54.8 reduce-scatter.1
  965.9 149.1 all-reduce.10
where the time goes:
time: 1120 us
  waiting for transfers between devices  1030 us (92%)
  other arithmetic  47.4 us (4%)
  matrix products  22.3 us (2%)
  between operations  14.2 us (1%)
    psum x1, waiting for transfers between devices, on_device(): full_first = lax.psum(solved, ('grp', 'row'))  271 us
    psum x1, waiting for transfers between devices, on_device(): gram_total = lax.psum(gram_local, ('grp', 'row'))  255 us
    psum x1, waiting for transfers between devices, on_device(): gram_second_total = lax.psum(gram_next, ('grp', 'row'))  254 us
    psum x1, waiting for transfers between devices, reduce_final(): return lax.psum(within, 'grp')  151 us
    reduce_scatter x1, waiting for transfers between devices, reduce_final(): within = lax.psum_scatter(summand, 'row', scatter_dimension=1, tiled=True)  54.9 us
    all_gather x1, waiting for transfers between devices, on_device(): lax.all_gather(probe_matrix, 'row', axis=1, tiled=True)  47.5 us
    another operation x6, other arithmetic, solve_lower(): factor = jnp.linalg.cholesky(gram_term)  24.8 us
  transfers between devices with their start and end apart: 6, of which 6 were waited for; matrix products, arithmetic and copies ran while one was open for 1% of the time, Pallas kernels for 0%

commit v1 on v0

v1 whole, which is shorter than its diff:
```python
import jax
import jax.numpy as jnp
from jax import lax
from jax.experimental import pallas as pl
from jax.experimental.pallas import tpu as pltpu
from jax.sharding import PartitionSpec as P

MESH = pl.DeviceIdType.MESH
NX, NY, NZ = 4, 8, 8
ROW = 2 * NZ
K = 128
TOK = 512
D = 4096
F32, BF16 = jnp.float32, jnp.bfloat16
NT = (((1,), (1,)), ((), ()))


def each(low, high, body):
    def step(i, carry):
        body(i)
        return carry

    lax.fori_loop(low, high, step, 0)


def kernel(
    act_hbm, probe_hbm, out_first, out_second,
    act, p_own, p_rel, q_own, q_rel, acc, acc_t, sk,
    g_loc, g_r1, g_s1, g_r2, g_s2, g_r3, g_full, elim_g, elim_x, linv,
    sib_out, sib_in, part, s1, r1a, r1b, t0, t1, r2, u, r3,
    bt, first, second,
    in_sem, probe_sem, gram_sem, cross_sem, gather_sem,
):
    grp, row = lax.axis_index("grp"), lax.axis_index("row")
    y, x = lax.div(grp, NX), lax.rem(grp, NX)
    z, c = lax.div(row, 2), lax.rem(row, 2)

    def z_dev(d):
        return (grp, lax.rem(z + d, NZ) * 2 + c)

    def y_dev(d):
        return (lax.rem(y + d, NY) * NX + x, row)

    def x_dev(d):
        return (y * NX + lax.rem(x + d, NX), row)

    def r_dev(d):
        return (grp, lax.rem(row + d, ROW))

    sib = (grp, row + 1 - 2 * c)

    def send(src, dst, sems, dev):
        pltpu.make_async_remote_copy(
            src_ref=src, dst_ref=dst, send_sem=sems.at[0], recv_sem=sems.at[1],
            device_id=dev, device_id_type=MESH,
        ).start()

    sent = []

    def arrived(ref, sems):
        pltpu.make_async_copy(ref, ref, sems.at[1]).wait()
        sent.append((ref, sems))

    load_act = pltpu.make_async_copy(act_hbm, act, in_sem.at[0])
    load_probe = pltpu.make_async_copy(probe_hbm, p_own, in_sem.at[1])
    load_probe.start()
    load_act.start()

    barrier = pltpu.get_barrier_semaphore()

    def greet(dev):
        pl.semaphore_signal(barrier, inc=1, device_id=dev, device_id_type=MESH)

    each(1, ROW, lambda d: greet(r_dev(d)))
    each(1, NY, lambda d: greet(y_dev(d)))
    each(1, NX, lambda d: greet(x_dev(d)))
    load_probe.wait()
    pl.semaphore_wait(barrier, ROW - 1 + NY - 1 + NX - 1)

    rows_y = pl.ds(pl.multiple_of(lax.rem(y, 4) * 32, 32), 32)
    rows_x = pl.ds(pl.multiple_of(x * 32, 32), 32)
    low, high = pl.ds(0, 128), pl.ds(128, 128)

    def probe_z(d):
        send(p_own.at[rows_y, low], p_rel.at[7 - d, rows_y, low], probe_sem.at[0], z_dev(d))
        send(p_own.at[rows_x, high], p_rel.at[7 - d, rows_x, high], probe_sem.at[1], z_dev(d))

    each(1, NZ, probe_z)
    send(p_own, q_own, probe_sem.at[2], sib)

    def columns(at, width):
        return pl.ds(pl.multiple_of(at, width), width)

    def probe_dot(block, z_at, c_at):
        return lax.dot_general(
            block, act[:, columns((z_at * 2 + c_at) * 256, 256)], NT, preferred_element_type=F32
        )

    arrived(p_rel.at[:, pl.ds(0, 32), low], probe_sem.at[0])
    for d in (1, 7, 2 + 4 * c):
        send(p_rel.at[:, rows_y, low], p_rel.at[:, rows_y, low], probe_sem.at[3], y_dev(d))
    arrived(p_rel.at[:, pl.ds(0, 32), high], probe_sem.at[1])
    for d in (1, 2, 3):
        send(p_rel.at[:, rows_x, high], p_rel.at[:, rows_x, high], probe_sem.at[4], x_dev(d))
    load_act.wait()
    acc[...] = probe_dot(p_own[...], z, c)
    arrived(q_own, probe_sem.at[2])
    acc[...] += probe_dot(q_own[...], z, 1 - c)
    arrived(p_rel.at[:, pl.ds(0, 96), high], probe_sem.at[4])
    send(p_rel.at[:, :, high], q_rel.at[:, :, high], probe_sem.at[5], sib)
    arrived(p_rel.at[:, pl.ds(0, 96), low], probe_sem.at[3])
    send(p_rel.at[:, :, low], q_rel.at[:, :, low], probe_sem.at[6], sib)

    def add_own(d):
        acc[...] += probe_dot(p_rel[d], lax.rem(z + d + 1, NZ), c)

    def add_sib(d):
        acc[...] += probe_dot(q_rel[d], lax.rem(z + d + 1, NZ), 1 - c)

    each(0, NZ - 1, add_own)
    arrived(q_rel.at[:, :, high], probe_sem.at[5])
    arrived(q_rel.at[:, :, low], probe_sem.at[6])
    each(0, NZ - 1, add_sib)
    sk[...] = acc[...].astype(BF16)

    def eliminate(count, rows, start):
        def step(i, carry):
            left, right = elim_g[0:rows, :], elim_x[0:rows, :]
            cols = [jnp.broadcast_to(left[:, j : j + 1], (rows, K)) for j in range(8)]
            g_rows = [left[j : j + 1, :] for j in range(8)]
            x_rows = [right[j : j + 1, :] for j in range(8)]
            for k in range(8):
                scale = lax.rsqrt(cols[k][k : k + 1, :])
                cols[k] = cols[k] * scale
                g_rows[k] = g_rows[k] * scale
                x_rows[k] = x_rows[k] * scale
                for j in range(k + 1, 8):
                    factor = cols[k][j : j + 1, :]
                    cols[j] = cols[j] - cols[k] * factor
                    g_rows[j] = g_rows[j] - g_rows[k] * factor
                    x_rows[j] = x_rows[j] - x_rows[k] * factor
            linv[pl.ds(pl.multiple_of((start + i) * 8, 8), 8), :] = jnp.concatenate(x_rows, axis=0)
            below = [col[8:, :] for col in cols]
            left, right = left[8:, :], right[8:, :]
            for k in range(8):
                left = left - below[k] * g_rows[k]
                right = right - below[k] * x_rows[k]
            elim_g[0 : rows - 8, :] = pltpu.roll(left, K - 8, 1)
            elim_x[0 : rows - 8, :] = right
            return carry

        lax.fori_loop(0, count, step, 0)

    def solve_round(rd, a_at, b_at, a_dev, b_dev):
        gram = gram_sem.at[rd]
        cross = cross_sem.at[rd]
        sketch = sk[...]
        g_loc[rd] = lax.dot_general(sketch, sketch, NT, preferred_element_type=F32).reshape(ROW, 8, K)
        each(1, ROW, lambda d: send(
            g_loc.at[rd, lax.rem(row + d, ROW)], g_r1.at[rd, d - 1], gram.at[0], r_dev(d)))

        def for_sibling(a):
            term = jnp.dot(
                sk[...], act[:, columns(a * 512 + (1 - c) * 256, 256)], preferred_element_type=F32
            )
            sib_out[rd, a] = term.T.astype(BF16)
            send(sib_out.at[rd, a], sib_in.at[rd, a], cross.at[0], sib)

        def for_self(a):
            term = jnp.dot(
                sk[...], act[:, columns(a * 512 + c * 256, 256)], preferred_element_type=F32
            )
            part[a] = term.T.reshape(2, 8, 16, K)

        each(0, 8, for_sibling)
        arrived(g_r1.at[rd], gram.at[0])
        total = g_loc[rd, row]
        for d in range(ROW - 1):
            total = total + g_r1[rd, d]
        g_s1[rd] = total
        each(1, NY, lambda d: send(g_s1.at[rd], g_r2.at[rd, d - 1], gram.at[1], y_dev(d)))
        each(0, 4, for_self)
        arrived(g_r2.at[rd], gram.at[1])
        for d in range(NY - 1):
            total = total + g_r2[rd, d]
        g_s2[rd] = total
        each(1, NX, lambda d: send(g_s2.at[rd], g_r3.at[rd, d - 1], gram.at[2], x_dev(d)))
        each(4, 8, for_self)
        arrived(g_r3.at[rd], gram.at[2])
        for d in range(NX - 1):
            total = total + g_r3[rd, d]
        g_full[rd, row] = total
        each(1, ROW, lambda d: send(g_full.at[rd, row], g_full.at[rd, row], gram.at[3], r_dev(d)))

        arrived(sib_in.at[rd], cross.at[0])

        def combine(a):
            both = part[a] + sib_in[rd, a].astype(F32).reshape(2, 8, 16, K)
            part[a] = both
            s1[rd, a] = both.astype(BF16)

        each(0, 8, combine)
        each(1, 8, lambda d: send(
            s1.at[rd, lax.rem(a_at + d, 8), 0], r1a.at[rd, d - 1], cross.at[1], a_dev(d)))
        each(1, 8, lambda d: send(
            s1.at[rd, :, 1, lax.rem(b_at + d, 8)], r1b.at[rd, d - 1], cross.at[2], b_dev(d)))

        arrived(g_full.at[rd, pl.ds(0, ROW - 1)], gram.at[3])
        elim_g[...] = g_full[rd].reshape(K, K)
        elim_x[...] = (
            lax.broadcasted_iota(jnp.int32, (K, K), 0) == lax.broadcasted_iota(jnp.int32, (K, K), 1)
        ).astype(F32)
        eliminate(4, 128, 0)
        eliminate(4, 96, 4)

        arrived(r1a.at[rd], cross.at[1])
        total_0 = part[a_at, 0]
        for d in range(7):
            total_0 = total_0 + r1a[rd, d].astype(F32)
        t0[rd] = total_0
        each(1, 8, lambda d: send(
            t0.at[rd, lax.rem(b_at + d, 8)], r2.at[rd, 0, d - 1], cross.at[3], b_dev(d)))
        arrived(r1b.at[rd], cross.at[2])
        total_1 = part[:, 1, b_at]
        for d in range(7):
            total_1 = total_1 + r1b[rd, d].astype(F32)
        t1[rd] = total_1
        each(1, 8, lambda d: send(
            t1.at[rd, lax.rem(a_at + d, 8)], r2.at[rd, 1, d - 1], cross.at[4], a_dev(d)))
        eliminate(4, 64, 8)
        arrived(r2.at[rd, 0], cross.at[3])
        arrived(r2.at[rd, 1], cross.at[4])
        sum_0, sum_1 = t0[rd, b_at], t1[rd, a_at]
        for d in range(7):
            sum_0 = sum_0 + r2[rd, 0, d]
            sum_1 = sum_1 + r2[rd, 1, d]
        u[rd, 0] = sum_0
        u[rd, 1] = sum_1
        each(1, NX, lambda d: send(u.at[rd], r3.at[rd, d - 1], cross.at[5], x_dev(d)))
        eliminate(4, 32, 12)
        arrived(r3.at[rd], cross.at[5])
        whole = u[rd]
        for d in range(NX - 1):
            whole = whole + r3[rd, d]
        solved = lax.dot_general(
            whole.reshape(32, K), linv[...], NT, precision=lax.Precision.HIGHEST,
            preferred_element_type=F32,
        )
        return solved.reshape(2, 16, K)

    solved = solve_round(0, y, z, y_dev, z_dev)
    first[c] = solved
    for h in range(2):
        bt[y, 2 * c + h, z] = solved[h].astype(BF16)
    each(1, NZ, lambda d: send(bt.at[y, 2 * c, z], bt.at[y, 2 * c, z], gather_sem.at[0], z_dev(d)))
    each(1, NY, lambda d: send(bt.at[y, 2 * c + 1, z], bt.at[y, 2 * c + 1, z], gather_sem.at[1], y_dev(d)))
    arrived(bt.at[0, 0, pl.ds(0, 7)], gather_sem.at[0])
    each(1, NY, lambda d: send(bt.at[y, 2 * c], bt.at[y, 2 * c], gather_sem.at[2], y_dev(d)))
    arrived(bt.at[0, 0, pl.ds(0, 7)], gather_sem.at[1])
    each(1, NZ, lambda d: send(bt.at[:, 2 * c + 1, z], bt.at[:, 2 * c + 1, z], gather_sem.at[3], z_dev(d)))
    send(first.at[c], first.at[c], gather_sem.at[6], sib)
    arrived(bt.at[pl.ds(0, 7), 0], gather_sem.at[2])
    send(bt.at[:, 2 * c], bt.at[:, 2 * c], gather_sem.at[4], sib)
    arrived(bt.at[pl.ds(0, 7), 0], gather_sem.at[3])
    send(bt.at[:, 2 * c + 1], bt.at[:, 2 * c + 1], gather_sem.at[5], sib)

    def back_dot(a, c_at):
        return jnp.dot(
            act[:, columns(a * 512 + c_at * 256, 256)],
            bt[a, pl.ds(2 * c_at, 2)].reshape(256, K),
            preferred_element_type=F32,
        )

    acc_t[...] = back_dot(0, c)

    def add_back(c_at):
        def add(a):
            acc_t[...] += back_dot(a, c_at)

        return add

    each(1, 8, add_back(c))
    arrived(bt.at[:, 0], gather_sem.at[4])
    arrived(bt.at[:, 0], gather_sem.at[5])
    each(0, 8, add_back(1 - c))
    sk[...] = acc_t[...].T.astype(BF16)

    solved = solve_round(1, z, y, z_dev, y_dev)
    second[:, y] = solved
    each(1, NY, lambda d: send(second.at[:, y], second.at[:, y], gather_sem.at[7], y_dev(d)))
    arrived(first.at[0], gather_sem.at[6])
    out_first[...] = first[lax.div(x, 2), lax.rem(x, 2), pl.ds(pl.multiple_of(8 * c, 8), 8), :]
    arrived(second.at[:, pl.ds(0, 7)], gather_sem.at[7])
    out_second[...] = second[...].reshape(256, K)
    for ref, sems in sent:
        pltpu.make_async_copy(ref, ref, sems.at[0]).wait()


def on_device(activations, probe_matrix):
    vmem = pltpu.VMEM
    first_t, second_t = pl.pallas_call(
        kernel,
        out_shape=(
            jax.ShapeDtypeStruct((8, K), F32),
            jax.ShapeDtypeStruct((256, K), F32),
        ),
        in_specs=[pl.BlockSpec(memory_space=pl.ANY)] * 2,
        out_specs=(
            pl.BlockSpec(memory_space=pltpu.VMEM),
            pl.BlockSpec(memory_space=pltpu.VMEM),
        ),
        scratch_shapes=[
            vmem((TOK, D), BF16),
            vmem((K, 256), BF16),
            vmem((7, K, 256), BF16),
            vmem((K, 256), BF16),
            vmem((7, K, 256), BF16),
            vmem((K, TOK), F32),
            vmem((TOK, K), F32),
            vmem((K, TOK), BF16),
            vmem((2, ROW, 8, K), F32),
            vmem((2, ROW - 1, 8, K), F32),
            vmem((2, 8, K), F32),
            vmem((2, NY - 1, 8, K), F32),
            vmem((2, 8, K), F32),
            vmem((2, NX - 1, 8, K), F32),
            vmem((2, ROW, 8, K), F32),
            vmem((K, K), F32),
            vmem((K, K), F32),
            vmem((K, K), F32),
            vmem((2, 8, 256, K), BF16),
            vmem((2, 8, 256, K), BF16),
            vmem((8, 2, 8, 16, K), F32),
            vmem((2, 8, 2, 8, 16, K), BF16),
            vmem((2, 7, 8, 16, K), BF16),
            vmem((2, 7, 8, 16, K), BF16),
            vmem((2, 8, 16, K), F32),
            vmem((2, 8, 16, K), F32),
            vmem((2, 2, 7, 16, K), F32),
            vmem((2, 2, 16, K), F32),
            vmem((2, NX - 1, 2, 16, K), F32),
            vmem((8, 4, 8, 16, K), BF16),
            vmem((2, 2, 16, K), F32),
            vmem((2, 8, 16, K), F32),
            pltpu.SemaphoreType.DMA((2,)),
            pltpu.SemaphoreType.DMA((7, 2)),
            pltpu.SemaphoreType.DMA((2, 4, 2)),
            pltpu.SemaphoreType.DMA((2, 6, 2)),
            pltpu.SemaphoreType.DMA((8, 2)),
        ],
        compiler_params=pltpu.CompilerParams(
            collective_id=0, has_side_effects=True, vmem_limit_bytes=48 * 1024 * 1024
        ),
        name="range_finder",
    )(activations, probe_matrix)
    return first_t.T, second_t.T


def solution(mesh):
    return jax.shard_map(
        on_device,
        mesh=mesh,
        in_specs=(P(("grp", "row"), None), P(None, "row")),
        out_specs=(P(None, ("grp", "row")), P(None, "row")),
        check_vma=False,
    )
```

time: 1120 us -> 119 us (0.11)
  the two profiles are of different devices: /device:TPU:14 before, /device:TPU:2 now
where the time goes in v1:
time: 119 us
  Pallas kernels  114 us (96%)
  local copies, waits for them, and re-layouts  4.37 us (4%)
    pallas_call x1, Pallas kernels, on_device(): pl.pallas_call(kernel, out_shape=(jax.ShapeDtypeStruct((8, K), F32), jax....  114 us
    unnamed x6, local copies, waits for them, and re-layouts  4.37 us

profile of v1, /device:TPU:2, one launch (start us, length us, event | category | flops | bytes accessed | tf_op | source)
XLA Modules:
  0.0 118.6 jit_solution(1159068719353455313)
XLA Ops:
  0.6 0.0 copy-start
  0.6 2.2 %copy-done = bf16[512,4096]{1,0:T(8,128)(2,1)S(1)} copy-done((bf16[512,4096]{1,0:T(8,128)(2,1)S(1)}, bf16[512,4096]{1,0:T(8,128)(2,1)}, u32[]{:S(2)}) %copy-start) | copy-done | bytes 4194328
  2.8 0.0 copy-start.1
  2.8 0.8 copy-done.1
  3.7 113.6 %range_finder.1 = (f32[8,128]{1,0:T(8,128)S(1)}, f32[256,128]{1,0:T(8,128)S(1)}) custom-call(bf16[512,4096]{1,0:T(8,128)(2,1)S(1)} %copy-done, bf16[128,256]{1,0:T(8,128)(2,1)S(1)} %copy-done.1), custom_call_target="tpu_custom_call" | custom-call | tf_op jit(solution)/shard_map/range_finder/pallas_call | solution.py:301
  117.3 0.8 copy.4
  118.0 0.6 copy.6
Async XLA Ops:
  0.6 2.2 %copy-start = (bf16[512,4096]{1,0:T(8,128)(2,1)S(1)}, bf16[512,4096]{1,0:T(8,128)(2,1)}, u32[]{:S(2)}) copy-start(bf16[512,4096]{1,0:T(8,128)(2,1)} %act_hbm.1) | copy-start | bytes 12582916
  2.8 0.8 copy-start.1

commit v2 on v1

--- a/solution.py
+++ b/solution.py
@@ -25,11 +25,11 @@
 
 def kernel(
     act_hbm, probe_hbm, out_first, out_second,
-    act, p_own, p_rel, q_own, q_rel, acc, acc_t, sk,
+    act, p_own, p_rel, q_own, q_rel, acc_t, sk,
     g_loc, g_r1, g_s1, g_r2, g_s2, g_r3, g_full, elim_g, elim_x, linv,
     sib_out, sib_in, part, s1, r1a, r1b, t0, t1, r2, u, r3,
     bt, first, second,
-    in_sem, probe_sem, gram_sem, cross_sem, gather_sem,
+    in_sem, probe_sem, gram_sem, cross_sem, sib_sem, gather_sem, line_sem, pass_sem,
 ):
     grp, row = lax.axis_index("grp"), lax.axis_index("row")
     y, x = lax.div(grp, NX), lax.rem(grp, NX)
@@ -93,7 +93,7 @@
 
     def probe_dot(block, z_at, c_at):
         return lax.dot_general(
-            block, act[:, columns((z_at * 2 + c_at) * 256, 256)], NT, preferred_element_type=F32
+            act[:, columns((z_at * 2 + c_at) * 256, 256)], block, NT, preferred_element_type=F32
         )
 
     arrived(p_rel.at[:, pl.ds(0, 32), low], probe_sem.at[0])
@@ -103,53 +103,79 @@
     for d in (1, 2, 3):
         send(p_rel.at[:, rows_x, high], p_rel.at[:, rows_x, high], probe_sem.at[4], x_dev(d))
     load_act.wait()
-    acc[...] = probe_dot(p_own[...], z, c)
+    acc_t[...] = probe_dot(p_own[...], z, c)
     arrived(q_own, probe_sem.at[2])
-    acc[...] += probe_dot(q_own[...], z, 1 - c)
+    acc_t[...] += probe_dot(q_own[...], z, 1 - c)
     arrived(p_rel.at[:, pl.ds(0, 96), high], probe_sem.at[4])
     send(p_rel.at[:, :, high], q_rel.at[:, :, high], probe_sem.at[5], sib)
     arrived(p_rel.at[:, pl.ds(0, 96), low], probe_sem.at[3])
     send(p_rel.at[:, :, low], q_rel.at[:, :, low], probe_sem.at[6], sib)
 
     def add_own(d):
-        acc[...] += probe_dot(p_rel[d], lax.rem(z + d + 1, NZ), c)
+        acc_t[...] += probe_dot(p_rel[d], lax.rem(z + d + 1, NZ), c)
 
     def add_sib(d):
-        acc[...] += probe_dot(q_rel[d], lax.rem(z + d + 1, NZ), 1 - c)
+        acc_t[...] += probe_dot(q_rel[d], lax.rem(z + d + 1, NZ), 1 - c)
 
     each(0, NZ - 1, add_own)
     arrived(q_rel.at[:, :, high], probe_sem.at[5])
     arrived(q_rel.at[:, :, low], probe_sem.at[6])
     each(0, NZ - 1, add_sib)
-    sk[...] = acc[...].astype(BF16)
-
-    def eliminate(count, rows, start):
+    sk[...] = acc_t[...].T.astype(BF16)
+
+    sublane = lax.broadcasted_iota(jnp.int32, (8, K), 0)
+
+    def spread(line):
+        return jnp.broadcast_to(line, (8, K))
+
+    def block_step(left, right, at, lane):
+        rows = left.shape[0]
+        pivot = [spread(left[0:8, lane + j : lane + j + 1]) for j in range(8)]
+        d = [[spread(pivot[j][i : i + 1, :]) if i >= j else None for j in range(8)] for i in range(8)]
+        g = [spread(left[j : j + 1, :]) for j in range(8)]
+        x = [spread(right[j : j + 1, :]) for j in range(8)]
+        scale = []
+        for k in range(8):
+            scale.append(lax.rsqrt(d[k][k]))
+            for i in range(k + 1, 8):
+                d[i][k] = d[i][k] * scale[k]
+            for j in range(k + 1, 8):
+                for i in range(j, 8):
+                    d[i][j] = d[i][j] - d[i][k] * d[j][k]
+            g[k] = g[k] * scale[k]
+            x[k] = x[k] * scale[k]
+            for j in range(k + 1, 8):
+                g[j] = g[j] - d[j][k] * g[k]
+                x[j] = x[j] - d[j][k] * x[k]
+        done = x[0]
+        for k in range(1, 8):
+            done = jnp.where(sublane == k, x[k], done)
+        linv[pl.ds(pl.multiple_of(at * 8, 8), 8), :] = done
+        for k in range(7, -1, -1):
+            g[k] = g[k] * scale[k]
+            x[k] = x[k] * scale[k]
+            for j in range(k):
+                g[j] = g[j] - d[k][j] * g[k]
+                x[j] = x[j] - d[k][j] * x[k]
+        groups = (rows - 8) // 8
+        rest, right = left[8:, :].reshape(groups, 8, K), right[8:, :].reshape(groups, 8, K)
+        below = rest
+        for k in range(8):
+            col = jnp.broadcast_to(below[:, :, lane + k : lane + k + 1], (groups, 8, K))
+            rest = rest - col * g[k][None]
+            right = right - col * x[k][None]
+        return rest.reshape(rows - 8, K), right.reshape(rows - 8, K)
+
+    def eliminate(rows, start):
         def step(i, carry):
             left, right = elim_g[0:rows, :], elim_x[0:rows, :]
-            cols = [jnp.broadcast_to(left[:, j : j + 1], (rows, K)) for j in range(8)]
-            g_rows = [left[j : j + 1, :] for j in range(8)]
-            x_rows = [right[j : j + 1, :] for j in range(8)]
-            for k in range(8):
-                scale = lax.rsqrt(cols[k][k : k + 1, :])
-                cols[k] = cols[k] * scale
-                g_rows[k] = g_rows[k] * scale
-                x_rows[k] = x_rows[k] * scale
-                for j in range(k + 1, 8):
-                    factor = cols[k][j : j + 1, :]
-                    cols[j] = cols[j] - cols[k] * factor
-                    g_rows[j] = g_rows[j] - g_rows[k] * factor
-                    x_rows[j] = x_rows[j] - x_rows[k] * factor
-            linv[pl.ds(pl.multiple_of((start + i) * 8, 8), 8), :] = jnp.concatenate(x_rows, axis=0)
-            below = [col[8:, :] for col in cols]
-            left, right = left[8:, :], right[8:, :]
-            for k in range(8):
-                left = left - below[k] * g_rows[k]
-                right = right - below[k] * x_rows[k]
-            elim_g[0 : rows - 8, :] = pltpu.roll(left, K - 8, 1)
-            elim_x[0 : rows - 8, :] = right
+            left, right = block_step(left, right, start + 2 * i, 0)
+            left, right = block_step(left, right, start + 2 * i + 1, 8)
+            elim_g[0 : rows - 16, :] = pltpu.roll(left, K - 16, 1)
+            elim_x[0 : rows - 16, :] = right
             return carry
 
-        lax.fori_loop(0, count, step, 0)
+        lax.fori_loop(0, 2, step, 0)
 
     def solve_round(rd, a_at, b_at, a_dev, b_dev):
         gram = gram_sem.at[rd]
@@ -159,85 +185,90 @@
         each(1, ROW, lambda d: send(
             g_loc.at[rd, lax.rem(row + d, ROW)], g_r1.at[rd, d - 1], gram.at[0], r_dev(d)))
 
-        def for_sibling(a):
+        def for_sibling(d):
+            a = lax.rem(a_at + d, 8)
             term = jnp.dot(
                 sk[...], act[:, columns(a * 512 + (1 - c) * 256, 256)], preferred_element_type=F32
             )
-            sib_out[rd, a] = term.T.astype(BF16)
-            send(sib_out.at[rd, a], sib_in.at[rd, a], cross.at[0], sib)
-
-        def for_self(a):
+            sib_out[rd, d - 1] = term.T.astype(BF16)
+            send(sib_out.at[rd, d - 1], sib_in.at[rd, d - 1], sib_sem.at[rd, d - 1], sib)
+
+        def for_self(d):
+            a = lax.rem(a_at + d, 8)
             term = jnp.dot(
                 sk[...], act[:, columns(a * 512 + c * 256, 256)], preferred_element_type=F32
-            )
-            part[a] = term.T.reshape(2, 8, 16, K)
-
-        each(0, 8, for_sibling)
+            ).T
+            pltpu.make_async_copy(sib_in.at[rd, 0], sib_in.at[rd, 0], sib_sem.at[rd, d - 1, 1]).wait()
+            both = (term + sib_in[rd, d - 1].astype(F32)).reshape(2, 8, 16, K)
+            part[d - 1] = both
+            s1[rd, d - 1] = both.astype(BF16)
+
+        def for_other(d):
+            for_self(d)
+            send(s1.at[rd, d - 1, 0], r1a.at[rd, d - 1], cross.at[1], a_dev(d))
+
+        def along_b(half):
+            each(1, 8, lambda d: send(
+                s1.at[rd, pl.ds(4 * half, 4), 1, lax.rem(b_at + d, 8)],
+                r1b.at[rd, half, d - 1], cross.at[6 * half], b_dev(d)))
+
+        each(1, 9, for_sibling)
         arrived(g_r1.at[rd], gram.at[0])
         total = g_loc[rd, row]
         for d in range(ROW - 1):
             total = total + g_r1[rd, d]
         g_s1[rd] = total
         each(1, NY, lambda d: send(g_s1.at[rd], g_r2.at[rd, d - 1], gram.at[1], y_dev(d)))
-        each(0, 4, for_self)
+        each(1, 5, for_other)
+        along_b(0)
         arrived(g_r2.at[rd], gram.at[1])
         for d in range(NY - 1):
             total = total + g_r2[rd, d]
         g_s2[rd] = total
         each(1, NX, lambda d: send(g_s2.at[rd], g_r3.at[rd, d - 1], gram.at[2], x_dev(d)))
-        each(4, 8, for_self)
+        each(5, 8, for_other)
+        for_self(8)
+        along_b(1)
         arrived(g_r3.at[rd], gram.at[2])
         for d in range(NX - 1):
             total = total + g_r3[rd, d]
         g_full[rd, row] = total
         each(1, ROW, lambda d: send(g_full.at[rd, row], g_full.at[rd, row], gram.at[3], r_dev(d)))
 
-        arrived(sib_in.at[rd], cross.at[0])
-
-        def combine(a):
-            both = part[a] + sib_in[rd, a].astype(F32).reshape(2, 8, 16, K)
-            part[a] = both
-            s1[rd, a] = both.astype(BF16)
-
-        each(0, 8, combine)
-        each(1, 8, lambda d: send(
-            s1.at[rd, lax.rem(a_at + d, 8), 0], r1a.at[rd, d - 1], cross.at[1], a_dev(d)))
-        each(1, 8, lambda d: send(
-            s1.at[rd, :, 1, lax.rem(b_at + d, 8)], r1b.at[rd, d - 1], cross.at[2], b_dev(d)))
-
         arrived(g_full.at[rd, pl.ds(0, ROW - 1)], gram.at[3])
         elim_g[...] = g_full[rd].reshape(K, K)
         elim_x[...] = (
             lax.broadcasted_iota(jnp.int32, (K, K), 0) == lax.broadcasted_iota(jnp.int32, (K, K), 1)
         ).astype(F32)
-        eliminate(4, 128, 0)
-        eliminate(4, 96, 4)
+        eliminate(128, 0)
+        eliminate(96, 4)
 
         arrived(r1a.at[rd], cross.at[1])
-        total_0 = part[a_at, 0]
+        total_0 = part[7, 0]
         for d in range(7):
             total_0 = total_0 + r1a[rd, d].astype(F32)
         t0[rd] = total_0
         each(1, 8, lambda d: send(
             t0.at[rd, lax.rem(b_at + d, 8)], r2.at[rd, 0, d - 1], cross.at[3], b_dev(d)))
-        arrived(r1b.at[rd], cross.at[2])
-        total_1 = part[:, 1, b_at]
-        for d in range(7):
-            total_1 = total_1 + r1b[rd, d].astype(F32)
-        t1[rd] = total_1
+        for half in range(2):
+            arrived(r1b.at[rd, half], cross.at[6 * half])
+            total_1 = part[4 * half : 4 * half + 4, 1, b_at]
+            for d in range(7):
+                total_1 = total_1 + r1b[rd, half, d].astype(F32)
+            t1[rd, 4 * half : 4 * half + 4] = total_1
         each(1, 8, lambda d: send(
-            t1.at[rd, lax.rem(a_at + d, 8)], r2.at[rd, 1, d - 1], cross.at[4], a_dev(d)))
-        eliminate(4, 64, 8)
+            t1.at[rd, d - 1], r2.at[rd, 1, d - 1], cross.at[4], a_dev(d)))
+        eliminate(64, 8)
         arrived(r2.at[rd, 0], cross.at[3])
         arrived(r2.at[rd, 1], cross.at[4])
-        sum_0, sum_1 = t0[rd, b_at], t1[rd, a_at]
+        sum_0, sum_1 = t0[rd, b_at], t1[rd, 7]
         for d in range(7):
             sum_0 = sum_0 + r2[rd, 0, d]
             sum_1 = sum_1 + r2[rd, 1, d]
         u[rd, 0] = sum_0
         u[rd, 1] = sum_1
         each(1, NX, lambda d: send(u.at[rd], r3.at[rd, d - 1], cross.at[5], x_dev(d)))
-        eliminate(4, 32, 12)
+        eliminate(32, 12)
         arrived(r3.at[rd], cross.at[5])
         whole = u[rd]
         for d in range(NX - 1):
@@ -255,14 +286,25 @@
     each(1, NZ, lambda d: send(bt.at[y, 2 * c, z], bt.at[y, 2 * c, z], gather_sem.at[0], z_dev(d)))
     each(1, NY, lambda d: send(bt.at[y, 2 * c + 1, z], bt.at[y, 2 * c + 1, z], gather_sem.at[1], y_dev(d)))
     arrived(bt.at[0, 0, pl.ds(0, 7)], gather_sem.at[0])
-    each(1, NY, lambda d: send(bt.at[y, 2 * c], bt.at[y, 2 * c], gather_sem.at[2], y_dev(d)))
+    each(1, NY, lambda d: send(bt.at[y, 2 * c], bt.at[y, 2 * c], line_sem.at[0, d - 1], y_dev(NY - d)))
+    send(bt.at[y, 2 * c], bt.at[y, 2 * c], pass_sem.at[0, 7], sib)
     arrived(bt.at[0, 0, pl.ds(0, 7)], gather_sem.at[1])
-    each(1, NZ, lambda d: send(bt.at[:, 2 * c + 1, z], bt.at[:, 2 * c + 1, z], gather_sem.at[3], z_dev(d)))
+    each(1, NZ, lambda d: send(
+        bt.at[:, 2 * c + 1, z], bt.at[:, 2 * c + 1, z], line_sem.at[1, d - 1], z_dev(NZ - d)))
+    send(bt.at[:, 2 * c + 1, z], bt.at[:, 2 * c + 1, z], pass_sem.at[1, 7], sib)
     send(first.at[c], first.at[c], gather_sem.at[6], sib)
-    arrived(bt.at[pl.ds(0, 7), 0], gather_sem.at[2])
-    send(bt.at[:, 2 * c], bt.at[:, 2 * c], gather_sem.at[4], sib)
-    arrived(bt.at[pl.ds(0, 7), 0], gather_sem.at[3])
-    send(bt.at[:, 2 * c + 1], bt.at[:, 2 * c + 1], gather_sem.at[5], sib)
+    piece = bt.at[0, 0]
+
+    def forward(d):
+        pltpu.make_async_copy(piece, piece, line_sem.at[0, d - 1, 1]).wait()
+        at_y = bt.at[lax.rem(y + d, NY), 2 * c]
+        send(at_y, at_y, pass_sem.at[0, d - 1], sib)
+        pltpu.make_async_copy(piece, piece, line_sem.at[1, d - 1, 1]).wait()
+        at_z = bt.at[:, 2 * c + 1, lax.rem(z + d, NZ)]
+        send(at_z, at_z, pass_sem.at[1, d - 1], sib)
+
+    for d in (1, 7, 2, 6, 3, 5, 4):
+        forward(d)
 
     def back_dot(a, c_at):
         return jnp.dot(
@@ -280,8 +322,12 @@
         return add
 
     each(1, 8, add_back(c))
-    arrived(bt.at[:, 0], gather_sem.at[4])
-    arrived(bt.at[:, 0], gather_sem.at[5])
+
+    def passed(d):
+        pltpu.make_async_copy(piece, piece, pass_sem.at[0, d, 1]).wait()
+        pltpu.make_async_copy(piece, piece, pass_sem.at[1, d, 1]).wait()
+
+    each(0, 8, passed)
     each(0, 8, add_back(1 - c))
     sk[...] = acc_t[...].T.astype(BF16)
 
@@ -295,6 +341,19 @@
     for ref, sems in sent:
         pltpu.make_async_copy(ref, ref, sems.at[0]).wait()
 
+    def left_behind(d):
+        for i in range(2):
+            pltpu.make_async_copy(sib_in.at[i, 0], sib_in.at[i, 0], sib_sem.at[i, d, 0]).wait()
+            pltpu.make_async_copy(piece, piece, pass_sem.at[i, d, 0]).wait()
+
+    each(0, 8, left_behind)
+
+    def line_left(d):
+        for i in range(2):
+            pltpu.make_async_copy(piece, piece, line_sem.at[i, d, 0]).wait()
+
+    each(0, 7, line_left)
+
 
 def on_device(activations, probe_matrix):
     vmem = pltpu.VMEM
@@ -304,7 +363,7 @@
             jax.ShapeDtypeStruct((8, K), F32),
             jax.ShapeDtypeStruct((256, K), F32),
         ),
-        in_specs=[pl.BlockSpec(memory_space=pl.ANY)] * 2,
+        in_specs=[pl.BlockSpec(memory_space=pltpu.HBM)] * 2,
         out_specs=(
             pl.BlockSpec(memory_space=pltpu.VMEM),
             pl.BlockSpec(memory_space=pltpu.VMEM),
@@ -315,7 +374,6 @@
             vmem((7, K, 256), BF16),
             vmem((K, 256), BF16),
             vmem((7, K, 256), BF16),
-            vmem((K, TOK), F32),
             vmem((TOK, K), F32),
             vmem((K, TOK), BF16),
             vmem((2, ROW, 8, K), F32),
@@ -333,7 +391,7 @@
             vmem((8, 2, 8, 16, K), F32),
             vmem((2, 8, 2, 8, 16, K), BF16),
             vmem((2, 7, 8, 16, K), BF16),
-            vmem((2, 7, 8, 16, K), BF16),
+            vmem((2, 2, 7, 4, 16, K), BF16),
             vmem((2, 8, 16, K), F32),
             vmem((2, 8, 16, K), F32),
             vmem((2, 2, 7, 16, K), F32),
@@ -345,11 +403,14 @@
             pltpu.SemaphoreType.DMA((2,)),
             pltpu.SemaphoreType.DMA((7, 2)),
             pltpu.SemaphoreType.DMA((2, 4, 2)),
-            pltpu.SemaphoreType.DMA((2, 6, 2)),
+            pltpu.SemaphoreType.DMA((2, 7, 2)),
+            pltpu.SemaphoreType.DMA((2, 8, 2)),
             pltpu.SemaphoreType.DMA((8, 2)),
+            pltpu.SemaphoreType.DMA((2, 7, 2)),
+            pltpu.SemaphoreType.DMA((2, 8, 2)),
         ],
         compiler_params=pltpu.CompilerParams(
-            collective_id=0, has_side_effects=True, vmem_limit_bytes=48 * 1024 * 1024
+            collective_id=0, has_side_effects=True, vmem_limit_bytes=58 * 1024 * 1024
         ),
         name="range_finder",
     )(activations, probe_matrix)

time: 119 us -> 115 us (0.966)
  Pallas kernels: 114 us -> 111 us
  local copies, waits for them, and re-layouts: 4.37 us -> 2.94 us
    pallas_call x1, Pallas kernels: 114 us -> 111 us  [on_device(): pl.pallas_call(kernel, out_shape=(jax.ShapeDtypeStruct((8, K), F32), jax....]
    unnamed x6 -> x2, local copies, waits for them, and re-layouts: 4.37 us -> 2.94 us
where the time goes in v2:
time: 115 us
  Pallas kernels  111 us (97%)
  local copies, waits for them, and re-layouts  2.94 us (3%)
    pallas_call x1, Pallas kernels, on_device(): pl.pallas_call(kernel, out_shape=(jax.ShapeDtypeStruct((8, K), F32), jax....  111 us
    unnamed x2, local copies, waits for them, and re-layouts  2.94 us

profile of v2, /device:TPU:2, one launch (start us, length us, event | category | flops | bytes accessed | tf_op | source)
XLA Modules:
  0.0 114.6 jit_solution(14403426370103931438)
XLA Ops:
  0.6 111.1 %range_finder.1 = (f32[8,128]{1,0:T(8,128)}, f32[256,128]{1,0:T(8,128)}) custom-call(bf16[512,4096]{1,0:T(8,128)(2,1)} %act_hbm.1, bf16[128,256]{1,0:T(8,128)(2,1)} %probe_hbm.1), custom_call_target="tpu_custom_call" | custom-call | tf_op jit(solution)/shard_map/range_finder/pallas_call | solution.py:360
  111.7 1.7 %copy.4 = f32[128,256]{1,0:T(8,128)} copy(f32[128,256]{0,1:T(8,128)} %bitcast.2) | data formatting | bytes 262144
  113.4 1.3 %copy.6 = f32[128,8]{0,1:T(8,128)} copy(f32[128,8]{0,1:T(8,128)} %bitcast.3) | data formatting | bytes 8192

commit v3 on v2

v3 whole, which is shorter than its diff:
```python
import jax
import jax.numpy as jnp
from jax import lax
from jax.experimental import pallas as pl
from jax.experimental.pallas import tpu as pltpu
from jax.sharding import PartitionSpec as P

MESH = pl.DeviceIdType.MESH
NX, NY, NZ = 4, 8, 8
K = 128
TOK = 512
D = 4096
F32, BF16 = jnp.float32, jnp.bfloat16
NT = (((1,), (1,)), ((), ()))


def each(low, high, body):
    def step(i, carry):
        body(i)
        return carry

    lax.fori_loop(low, high, step, 0)


def kernel(
    act_hbm, probe_hbm, out_first, out_second,
    act, p_own, p_full, half_out, half_in, sk,
    g_loc, g_r1, g_r2, g_full, elim_g, elim_x, linv,
    part, s1, r1a, r1b, t0, t1, r2, r3,
    bt, first, second,
    in_sem, probe_sem, half_sem, gram_sem, cross_sem, gather_sem,
):
    grp, row = lax.axis_index("grp"), lax.axis_index("row")
    y, x = lax.div(grp, NX), lax.rem(grp, NX)
    z, c = lax.div(row, 2), lax.rem(row, 2)
    x0, x1 = lax.rem(x, 2), lax.div(x, 2)

    def z_dev(d):
        return (grp, lax.rem(z + d, NZ) * 2 + c)

    def y_dev(d):
        return (lax.rem(y + d, NY) * NX + x, row)

    def x_dev(d):
        return (y * NX + lax.rem(x + d, NX), row)

    g_at, t_at = z * 2 + x0, y * 2 + x1

    def scatter_dev(d):
        at = lax.rem(g_at + d, 16)
        return (y * NX + 2 * x1 + lax.rem(at, 2), lax.div(at, 2) * 2 + c)

    def total_dev(d):
        at = lax.rem(t_at + d, 16)
        return (lax.div(at, 2) * NX + 2 * lax.rem(at, 2) + x0, row)

    sib = (grp, row + 1 - 2 * c)

    def send(src, dst, sems, dev):
        pltpu.make_async_remote_copy(
            src_ref=src, dst_ref=dst, send_sem=sems.at[0], recv_sem=sems.at[1],
            device_id=dev, device_id_type=MESH,
        ).start()

    sent = []

    def arrived(ref, sems):
        pltpu.make_async_copy(ref, ref, sems.at[1]).wait()
        sent.append((ref, sems))

    def columns(at, width):
        return pl.ds(pl.multiple_of(at, width), width)

    rows_y = columns(lax.rem(y, 4) * 16, 16)
    rows_x = columns(64 + x * 16, 16)
    mine = columns(c * TOK, TOK)
    load_probe = pltpu.make_async_copy(probe_hbm, p_own, in_sem.at[1])
    load_probe.start()
    for rows in (rows_y, rows_x):
        pltpu.make_async_copy(probe_hbm.at[rows], p_full.at[rows, columns(z * 256, 256)], in_sem.at[2]).start()

    def load(a):
        pltpu.make_async_copy(
            act_hbm.at[:, columns(a * 512 + c * 256, 256)], act.at[mine, columns(a * 256, 256)], in_sem.at[0]
        ).start()

    each(0, 8, load)

    barrier = pltpu.get_barrier_semaphore()

    def greet(dev):
        pl.semaphore_signal(barrier, inc=1, device_id=dev, device_id_type=MESH)

    each(1, 16, lambda d: greet(scatter_dev(d)))
    each(1, 16, lambda d: greet(total_dev(d)))
    greet((y * NX + 3 - x, row))
    greet(sib)
    load_probe.wait()
    pl.semaphore_wait(barrier, 32)

    def probe_z(d):
        for rows, sems in ((rows_y, probe_sem.at[0]), (rows_x, probe_sem.at[1])):
            send(p_own.at[rows], p_full.at[rows, columns(z * 256, 256)], sems, z_dev(d))

    each(1, NZ, probe_z)

    def push(a):
        send(
            act_hbm.at[:, columns(a * 512 + (1 - c) * 256, 256)],
            act.at[mine, columns(a * 256, 256)], probe_sem.at[2], sib)

    each(0, 8, push)
    two = p_full.at[pl.ds(0, 32), pl.ds(0, 256)]
    pltpu.make_async_copy(two, two, in_sem.at[2]).wait()
    seven = p_full.at[pl.ds(0, 16), pl.ds(0, 7 * 256)]
    arrived(seven, probe_sem.at[0])
    for d in (1, 7, 2 + 4 * c):
        send(p_full.at[rows_y], p_full.at[rows_y], probe_sem.at[3], y_dev(d))
    arrived(seven, probe_sem.at[1])
    for d in (1, 2, 3):
        send(p_full.at[rows_x], p_full.at[rows_x], probe_sem.at[4], x_dev(d))
    own_half = act.at[pl.ds(0, TOK)]
    pltpu.make_async_copy(own_half, own_half, in_sem.at[0]).wait()
    arrived(own_half, probe_sem.at[2])
    arrived(p_full.at[pl.ds(0, 48)], probe_sem.at[3])
    arrived(p_full.at[pl.ds(0, 48)], probe_sem.at[4])

    def both_halves(rd, product):
        def partial(q):
            half_out[rd, q] = product(act[columns(q * 256, 256), :])
            send(half_out.at[rd, q], half_in.at[rd, q], half_sem.at[rd, q], sib)

        each(0, 4, partial)
        for q in range(4):
            arrived(half_in.at[rd, q], half_sem.at[rd, q])
            sk[:, q * 256 : q * 256 + 256] = (half_out[rd, q] + half_in[rd, q]).T.astype(BF16)

    both_halves(0, lambda rows: lax.dot_general(rows, p_full[...], NT, preferred_element_type=F32))

    sublane = lax.broadcasted_iota(jnp.int32, (8, K), 0)

    def spread(line):
        return jnp.broadcast_to(line, (8, K))

    def block_step(left, right, at, lane):
        rows = left.shape[0]
        pivot = [spread(left[0:8, lane + j : lane + j + 1]) for j in range(8)]
        d = [[spread(pivot[j][i : i + 1, :]) if i >= j else None for j in range(8)] for i in range(8)]
        g = [spread(left[j : j + 1, :]) for j in range(8)]
        x = [spread(right[j : j + 1, :]) for j in range(8)]
        scale = []
        for k in range(8):
            scale.append(lax.rsqrt(d[k][k]))
            for i in range(k + 1, 8):
                d[i][k] = d[i][k] * scale[k]
            for j in range(k + 1, 8):
                for i in range(j, 8):
                    d[i][j] = d[i][j] - d[i][k] * d[j][k]
            g[k] = g[k] * scale[k]
            x[k] = x[k] * scale[k]
            for j in range(k + 1, 8):
                g[j] = g[j] - d[j][k] * g[k]
                x[j] = x[j] - d[j][k] * x[k]
        done = x[0]
        for k in range(1, 8):
            done = jnp.where(sublane == k, x[k], done)
        linv[pl.ds(pl.multiple_of(at * 8, 8), 8), :] = done
        for k in range(7, -1, -1):
            g[k] = g[k] * scale[k]
            x[k] = x[k] * scale[k]
            for j in range(k):
                g[j] = g[j] - d[k][j] * g[k]
                x[j] = x[j] - d[k][j] * x[k]
        groups = (rows - 8) // 8
        rest, right = left[8:, :].reshape(groups, 8, K), right[8:, :].reshape(groups, 8, K)
        below = rest
        for k in range(8):
            col = jnp.broadcast_to(below[:, :, lane + k : lane + k + 1], (groups, 8, K))
            rest = rest - col * g[k][None]
            right = right - col * x[k][None]
        return rest.reshape(rows - 8, K), right.reshape(rows - 8, K)

    def eliminate(rows, start):
        def step(i, carry):
            left, right = elim_g[0:rows, :], elim_x[0:rows, :]
            left, right = block_step(left, right, start + 2 * i, 0)
            left, right = block_step(left, right, start + 2 * i + 1, 8)
            elim_g[0 : rows - 16, :] = pltpu.roll(left, K - 16, 1)
            elim_x[0 : rows - 16, :] = right
            return carry

        lax.fori_loop(0, 2, step, 0)

    def solve_round(rd, a_at, b_at, a_dev, b_dev):
        gram = gram_sem.at[rd]
        cross = cross_sem.at[rd]
        sketch = sk[...]
        g_loc[rd] = lax.dot_general(sketch, sketch, NT, preferred_element_type=F32).reshape(16, 8, K)
        each(1, 16, lambda d: send(
            g_loc.at[rd, lax.rem(g_at + d, 16)], g_r1.at[rd, d - 1], gram.at[0], scatter_dev(d)))

        def cross_of(d):
            a = lax.rem(a_at + d, 8)
            term = jnp.dot(sk[...], act[:, columns(a * 256, 256)], preferred_element_type=F32)
            term = term.T.reshape(2, 8, 16, K)
            part[d - 1] = term
            s1[rd, d - 1] = term.astype(BF16)

        def cross_to(d):
            cross_of(d)
            send(s1.at[rd, d - 1, 0], r1a.at[rd, d - 1], cross.at[1], a_dev(d))

        def along_b(half):
            each(1, 8, lambda d: send(
                s1.at[rd, pl.ds(4 * half, 4), 1, lax.rem(b_at + d, 8)],
                r1b.at[rd, half, d - 1], cross.at[2 * half], b_dev(d)))

        each(1, 5, cross_to)
        arrived(g_r1.at[rd], gram.at[0])
        total = g_loc[rd, g_at]
        for d in range(15):
            total = total + g_r1[rd, d]
        g_r2[rd, t_at] = total
        each(1, 16, lambda d: send(g_r2.at[rd, t_at], g_r2.at[rd, t_at], gram.at[1], total_dev(d)))
        along_b(0)
        each(5, 8, cross_to)
        cross_of(8)
        arrived(g_r2.at[rd, pl.ds(0, 15)], gram.at[1])
        total = g_r2[rd, 0]
        for d in range(1, 16):
            total = total + g_r2[rd, d]
        g_full[rd, g_at] = total
        each(1, 16, lambda d: send(
            g_full.at[rd, g_at], g_full.at[rd, g_at], gram.at[2], scatter_dev(d)))
        along_b(1)

        arrived(g_full.at[rd, pl.ds(0, 15)], gram.at[2])
        elim_g[...] = g_full[rd].reshape(K, K)
        elim_x[...] = (
            lax.broadcasted_iota(jnp.int32, (K, K), 0) == lax.broadcasted_iota(jnp.int32, (K, K), 1)
        ).astype(F32)
        eliminate(128, 0)
        eliminate(96, 4)

        arrived(r1a.at[rd], cross.at[1])
        total_0 = part[7, 0]
        for d in range(7):
            total_0 = total_0 + r1a[rd, d].astype(F32)
        t0[rd] = total_0
        each(1, 8, lambda d: send(
            t0.at[rd, lax.rem(b_at + d, 8)], r2.at[rd, 0, d - 1], cross.at[3], b_dev(d)))
        for half in range(2):
            arrived(r1b.at[rd, half], cross.at[2 * half])
            total_1 = part[4 * half : 4 * half + 4, 1, b_at]
            for d in range(7):
                total_1 = total_1 + r1b[rd, half, d].astype(F32)
            t1[rd, 4 * half : 4 * half + 4] = total_1
        each(1, 8, lambda d: send(
            t1.at[rd, d - 1], r2.at[rd, 1, d - 1], cross.at[4], a_dev(d)))
        eliminate(64, 8)
        arrived(r2.at[rd, 0], cross.at[3])
        arrived(r2.at[rd, 1], cross.at[4])
        sum_0, sum_1 = t0[rd, b_at], t1[rd, 7]
        for d in range(7):
            sum_0 = sum_0 + r2[rd, 0, d]
            sum_1 = sum_1 + r2[rd, 1, d]
        r3[rd, x, 0] = sum_0
        r3[rd, x, 1] = sum_1
        each(1, NX, lambda d: send(r3.at[rd, x], r3.at[rd, x], cross.at[5], x_dev(d)))
        eliminate(32, 12)
        arrived(r3.at[rd, pl.ds(0, NX - 1)], cross.at[5])
        whole = r3[rd, 0]
        for d in range(1, NX):
            whole = whole + r3[rd, d]
        solved = lax.dot_general(
            whole.reshape(32, K), linv[...], NT, precision=lax.Precision.HIGHEST,
            preferred_element_type=F32,
        )
        return solved.reshape(2, 16, K)

    solved = solve_round(0, y, z, y_dev, z_dev)
    first[c] = solved
    for h in range(2):
        bt[y, h, z] = solved[h].astype(BF16)
    each(1, NZ, lambda d: send(bt.at[y, 0, z], bt.at[y, 0, z], gather_sem.at[0], z_dev(d)))
    each(1, NY, lambda d: send(bt.at[y, 1, z], bt.at[y, 1, z], gather_sem.at[1], y_dev(d)))
    arrived(bt.at[0, 0, pl.ds(0, 7)], gather_sem.at[0])
    each(1, NY, lambda d: send(bt.at[y, 0], bt.at[y, 0], gather_sem.at[2], y_dev(d)))
    arrived(bt.at[pl.ds(0, 7), 0, 0], gather_sem.at[1])
    each(1, NZ, lambda d: send(bt.at[:, 1, z], bt.at[:, 1, z], gather_sem.at[3], z_dev(d)))
    send(first.at[c], first.at[c], gather_sem.at[4], sib)
    arrived(bt.at[pl.ds(0, 7), 0], gather_sem.at[2])
    arrived(bt.at[:, 0, pl.ds(0, 7)], gather_sem.at[3])
    both_halves(1, lambda rows: jnp.dot(
        rows, bt[...].reshape(2048, K), preferred_element_type=F32))

    solved = solve_round(1, z, y, z_dev, y_dev)
    second[:, y] = solved
    each(1, NY, lambda d: send(second.at[:, y], second.at[:, y], gather_sem.at[5], y_dev(d)))
    arrived(first.at[0], gather_sem.at[4])
    out_first[...] = first[lax.div(x, 2), lax.rem(x, 2), pl.ds(pl.multiple_of(8 * c, 8), 8), :]
    arrived(second.at[:, pl.ds(0, 7)], gather_sem.at[5])
    out_second[...] = second[...].reshape(256, K)
    for ref, sems in sent:
        pltpu.make_async_copy(ref, ref, sems.at[0]).wait()


def on_device(activations, probe_matrix):
    vmem = pltpu.VMEM
    first_t, second_t = pl.pallas_call(
        kernel,
        out_shape=(
            jax.ShapeDtypeStruct((8, K), F32),
            jax.ShapeDtypeStruct((256, K), F32),
        ),
        in_specs=[pl.BlockSpec(memory_space=pltpu.HBM)] * 2,
        out_specs=(
            pl.BlockSpec(memory_space=pltpu.VMEM),
            pl.BlockSpec(memory_space=pltpu.VMEM),
        ),
        scratch_shapes=[
            vmem((2 * TOK, D // 2), BF16),
            vmem((K, 256), BF16),
            vmem((K, D // 2), BF16),
            vmem((2, 4, 256, K), F32),
            vmem((2, 4, 256, K), F32),
            vmem((K, 2 * TOK), BF16),
            vmem((2, 16, 8, K), F32),
            vmem((2, 15, 8, K), F32),
            vmem((2, 16, 8, K), F32),
            vmem((2, 16, 8, K), F32),
            vmem((K, K), F32),
            vmem((K, K), F32),
            vmem((K, K), F32),
            vmem((8, 2, 8, 16, K), F32),
            vmem((2, 8, 2, 8, 16, K), BF16),
            vmem((2, 7, 8, 16, K), BF16),
            vmem((2, 2, 7, 4, 16, K), BF16),
            vmem((2, 8, 16, K), F32),
            vmem((2, 8, 16, K), F32),
            vmem((2, 2, 7, 16, K), F32),
            vmem((2, NX, 2, 16, K), F32),
            vmem((8, 2, 8, 16, K), BF16),
            vmem((2, 2, 16, K), F32),
            vmem((2, 8, 16, K), F32),
            pltpu.SemaphoreType.DMA((3,)),
            pltpu.SemaphoreType.DMA((5, 2)),
            pltpu.SemaphoreType.DMA((2, 4, 2)),
            pltpu.SemaphoreType.DMA((2, 3, 2)),
            pltpu.SemaphoreType.DMA((2, 6, 2)),
            pltpu.SemaphoreType.DMA((6, 2)),
        ],
        compiler_params=pltpu.CompilerParams(
            collective_id=0, has_side_effects=True, vmem_limit_bytes=58 * 1024 * 1024
        ),
        name="range_finder",
    )(activations, probe_matrix)
    return first_t.T, second_t.T


def solution(mesh):
    return jax.shard_map(
        on_device,
        mesh=mesh,
        in_specs=(P(("grp", "row"), None), P(None, "row")),
        out_specs=(P(None, ("grp", "row")), P(None, "row")),
        check_vma=False,
    )
```

time: 115 us -> 116 us (level)
  the two profiles are of different devices: /device:TPU:2 before, /device:TPU:16 now
where the time goes in v3:
time: 116 us
  Pallas kernels  112 us (97%)
  local copies, waits for them, and re-layouts  2.94 us (3%)
    pallas_call x1, Pallas kernels, on_device(): pl.pallas_call(kernel, out_shape=(jax.ShapeDtypeStruct((8, K), F32), jax....  112 us
    unnamed x2, local copies, waits for them, and re-layouts  2.94 us

profile of v3, /device:TPU:16, one launch (start us, length us, event | category | flops | bytes accessed | tf_op | source)
XLA Modules:
  0.0 115.6 jit_solution(3490764575792765513)
XLA Ops:
  0.6 112.0 %range_finder.1 = (f32[8,128]{1,0:T(8,128)}, f32[256,128]{1,0:T(8,128)}) custom-call(bf16[512,4096]{1,0:T(8,128)(2,1)} %act_hbm.1, bf16[128,256]{1,0:T(8,128)(2,1)} %probe_hbm.1), custom_call_target="tpu_custom_call" | custom-call | tf_op jit(solution)/shard_map/range_finder/pallas_call | solution.py:310
  112.6 1.7 %copy.4 = f32[128,256]{1,0:T(8,128)} copy(f32[128,256]{0,1:T(8,128)} %bitcast.2) | data formatting | bytes 262144
  114.3 1.3 %copy.6 = f32[128,8]{0,1:T(8,128)} copy(f32[128,8]{0,1:T(8,128)} %bitcast.3) | data formatting | bytes 8192

commit v4 on v3

--- a/solution.py
+++ b/solution.py
@@ -12,6 +12,7 @@
 D = 4096
 F32, BF16 = jnp.float32, jnp.bfloat16
 NT = (((1,), (1,)), ((), ()))
+FAR = (4, 3, 5, 2, 6, 1, 7)
 
 
 def each(low, high, body):
@@ -24,8 +25,8 @@
 
 def kernel(
     act_hbm, probe_hbm, out_first, out_second,
-    act, p_own, p_full, half_out, half_in, sk,
-    g_loc, g_r1, g_r2, g_full, elim_g, elim_x, linv,
+    act, p_in, p_own, p_line, p_full, half_out, half_in, sk,
+    g_loc, g_r1, g_r2, g_r3, g_full, elim_g, elim_x, linv,
     part, s1, r1a, r1b, t0, t1, r2, r3,
     bt, first, second,
     in_sem, probe_sem, half_sem, gram_sem, cross_sem, gather_sem,
@@ -33,7 +34,6 @@
     grp, row = lax.axis_index("grp"), lax.axis_index("row")
     y, x = lax.div(grp, NX), lax.rem(grp, NX)
     z, c = lax.div(row, 2), lax.rem(row, 2)
-    x0, x1 = lax.rem(x, 2), lax.div(x, 2)
 
     def z_dev(d):
         return (grp, lax.rem(z + d, NZ) * 2 + c)
@@ -43,16 +43,6 @@
 
     def x_dev(d):
         return (y * NX + lax.rem(x + d, NX), row)
-
-    g_at, t_at = z * 2 + x0, y * 2 + x1
-
-    def scatter_dev(d):
-        at = lax.rem(g_at + d, 16)
-        return (y * NX + 2 * x1 + lax.rem(at, 2), lax.div(at, 2) * 2 + c)
-
-    def total_dev(d):
-        at = lax.rem(t_at + d, 16)
-        return (lax.div(at, 2) * NX + 2 * lax.rem(at, 2) + x0, row)
 
     sib = (grp, row + 1 - 2 * c)
 
@@ -71,13 +61,9 @@
     def columns(at, width):
         return pl.ds(pl.multiple_of(at, width), width)
 
-    rows_y = columns(lax.rem(y, 4) * 16, 16)
-    rows_x = columns(64 + x * 16, 16)
     mine = columns(c * TOK, TOK)
-    load_probe = pltpu.make_async_copy(probe_hbm, p_own, in_sem.at[1])
+    load_probe = pltpu.make_async_copy(probe_hbm, p_in, in_sem.at[1])
     load_probe.start()
-    for rows in (rows_y, rows_x):
-        pltpu.make_async_copy(probe_hbm.at[rows], p_full.at[rows, columns(z * 256, 256)], in_sem.at[2]).start()
 
     def load(a):
         pltpu.make_async_copy(
@@ -91,18 +77,21 @@
     def greet(dev):
         pl.semaphore_signal(barrier, inc=1, device_id=dev, device_id_type=MESH)
 
-    each(1, 16, lambda d: greet(scatter_dev(d)))
-    each(1, 16, lambda d: greet(total_dev(d)))
-    greet((y * NX + 3 - x, row))
+    for d in (4, 3, 5, 2, 6, 1, 7):
+        greet(z_dev(d))
+        greet(y_dev(d))
+    for d in (2, 1, 3):
+        greet(x_dev(d))
     greet(sib)
     load_probe.wait()
-    pl.semaphore_wait(barrier, 32)
-
-    def probe_z(d):
-        for rows, sems in ((rows_y, probe_sem.at[0]), (rows_x, probe_sem.at[1])):
-            send(p_own.at[rows], p_full.at[rows, columns(z * 256, 256)], sems, z_dev(d))
-
-    each(1, NZ, probe_z)
+    p_own[...] = p_in[...].T.reshape(2, 4, 32, K)
+    y_part = lax.rem(y, 4)
+    p_line[z, 0] = p_own[0, y_part]
+    p_line[z, 1] = p_own[1, x]
+    pl.semaphore_wait(barrier, 18)
+
+    for d in (4, 3, 5, 2, 6, 1, 7):
+        send(p_line.at[z], p_line.at[z], probe_sem.at[0], z_dev(d))
 
     def push(a):
         send(
@@ -110,20 +99,18 @@
             act.at[mine, columns(a * 256, 256)], probe_sem.at[2], sib)
 
     each(0, 8, push)
-    two = p_full.at[pl.ds(0, 32), pl.ds(0, 256)]
-    pltpu.make_async_copy(two, two, in_sem.at[2]).wait()
-    seven = p_full.at[pl.ds(0, 16), pl.ds(0, 7 * 256)]
-    arrived(seven, probe_sem.at[0])
+    arrived(p_line.at[pl.ds(0, 7)], probe_sem.at[0])
     for d in (1, 7, 2 + 4 * c):
-        send(p_full.at[rows_y], p_full.at[rows_y], probe_sem.at[3], y_dev(d))
-    arrived(seven, probe_sem.at[1])
-    for d in (1, 2, 3):
-        send(p_full.at[rows_x], p_full.at[rows_x], probe_sem.at[4], x_dev(d))
+        send(p_line.at[:, 0], p_full.at[:, 0, y_part], probe_sem.at[3], y_dev(d))
+    for d in (2, 1, 3):
+        send(p_line.at[:, 1], p_full.at[:, 1, x], probe_sem.at[4], x_dev(d))
+    p_full[:, 0, y_part] = p_line[:, 0]
+    p_full[:, 1, x] = p_line[:, 1]
     own_half = act.at[pl.ds(0, TOK)]
     pltpu.make_async_copy(own_half, own_half, in_sem.at[0]).wait()
     arrived(own_half, probe_sem.at[2])
-    arrived(p_full.at[pl.ds(0, 48)], probe_sem.at[3])
-    arrived(p_full.at[pl.ds(0, 48)], probe_sem.at[4])
+    arrived(p_full.at[:, 0, pl.ds(0, 3)], probe_sem.at[3])
+    arrived(p_full.at[:, 0, pl.ds(0, 3)], probe_sem.at[4])
 
     def both_halves(rd, product):
         def partial(q):
@@ -135,15 +122,16 @@
             arrived(half_in.at[rd, q], half_sem.at[rd, q])
             sk[:, q * 256 : q * 256 + 256] = (half_out[rd, q] + half_in[rd, q]).T.astype(BF16)
 
-    both_halves(0, lambda rows: lax.dot_general(rows, p_full[...], NT, preferred_element_type=F32))
+    both_halves(0, lambda rows: jnp.dot(
+        rows, p_full[...].reshape(2048, K), preferred_element_type=F32))
 
     sublane = lax.broadcasted_iota(jnp.int32, (8, K), 0)
 
     def spread(line):
         return jnp.broadcast_to(line, (8, K))
 
-    def block_step(left, right, at, lane):
-        rows = left.shape[0]
+    def block_step(left, right, at):
+        rows, lane = left.shape[0], at * 8
         pivot = [spread(left[0:8, lane + j : lane + j + 1]) for j in range(8)]
         d = [[spread(pivot[j][i : i + 1, :]) if i >= j else None for j in range(8)] for i in range(8)]
         g = [spread(left[j : j + 1, :]) for j in range(8)]
@@ -164,7 +152,9 @@
         done = x[0]
         for k in range(1, 8):
             done = jnp.where(sublane == k, x[k], done)
-        linv[pl.ds(pl.multiple_of(at * 8, 8), 8), :] = done
+        linv[at * 8 : at * 8 + 8, :] = done
+        if rows == 8:
+            return None, None
         for k in range(7, -1, -1):
             g[k] = g[k] * scale[k]
             x[k] = x[k] * scale[k]
@@ -180,24 +170,22 @@
             right = right - col * x[k][None]
         return rest.reshape(rows - 8, K), right.reshape(rows - 8, K)
 
-    def eliminate(rows, start):
-        def step(i, carry):
-            left, right = elim_g[0:rows, :], elim_x[0:rows, :]
-            left, right = block_step(left, right, start + 2 * i, 0)
-            left, right = block_step(left, right, start + 2 * i + 1, 8)
-            elim_g[0 : rows - 16, :] = pltpu.roll(left, K - 16, 1)
-            elim_x[0 : rows - 16, :] = right
-            return carry
-
-        lax.fori_loop(0, 2, step, 0)
+    def eliminate(start):
+        rows = K - 8 * start
+        left, right = elim_g[0:rows, :], elim_x[0:rows, :]
+        for at in range(start, start + 4):
+            left, right = block_step(left, right, at)
+        if left is not None:
+            elim_g[0 : rows - 32, :] = left
+            elim_x[0 : rows - 32, :] = right
 
     def solve_round(rd, a_at, b_at, a_dev, b_dev):
         gram = gram_sem.at[rd]
         cross = cross_sem.at[rd]
         sketch = sk[...]
-        g_loc[rd] = lax.dot_general(sketch, sketch, NT, preferred_element_type=F32).reshape(16, 8, K)
-        each(1, 16, lambda d: send(
-            g_loc.at[rd, lax.rem(g_at + d, 16)], g_r1.at[rd, d - 1], gram.at[0], scatter_dev(d)))
+        g_loc[rd] = lax.dot_general(sketch, sketch, NT, preferred_element_type=F32).reshape(8, 16, K)
+        for d in FAR:
+            send(g_loc.at[rd, lax.rem(z + d, 8)], g_r1.at[rd, d - 1], gram.at[0], z_dev(d))
 
         def cross_of(d):
             a = lax.rem(a_at + d, 8)
@@ -217,30 +205,39 @@
 
         each(1, 5, cross_to)
         arrived(g_r1.at[rd], gram.at[0])
-        total = g_loc[rd, g_at]
-        for d in range(15):
+        total = g_loc[rd, z]
+        for d in range(7):
             total = total + g_r1[rd, d]
-        g_r2[rd, t_at] = total
-        each(1, 16, lambda d: send(g_r2.at[rd, t_at], g_r2.at[rd, t_at], gram.at[1], total_dev(d)))
+        g_r2[rd, y] = total
+        for d in FAR:
+            send(g_r2.at[rd, y], g_r2.at[rd, y], gram.at[1], y_dev(d))
+        each(5, 7, cross_to)
+        arrived(g_r2.at[rd, pl.ds(0, 7)], gram.at[1])
+        total = g_r2[rd, 0]
+        for d in range(1, 8):
+            total = total + g_r2[rd, d]
+        g_r3[rd, x] = total
+        for d in (2, 1, 3):
+            send(g_r3.at[rd, x], g_r3.at[rd, x], gram.at[2], x_dev(d))
         along_b(0)
-        each(5, 8, cross_to)
+        each(7, 8, cross_to)
         cross_of(8)
-        arrived(g_r2.at[rd, pl.ds(0, 15)], gram.at[1])
-        total = g_r2[rd, 0]
-        for d in range(1, 16):
-            total = total + g_r2[rd, d]
-        g_full[rd, g_at] = total
-        each(1, 16, lambda d: send(
-            g_full.at[rd, g_at], g_full.at[rd, g_at], gram.at[2], scatter_dev(d)))
+        arrived(g_r3.at[rd, pl.ds(0, 3)], gram.at[2])
+        total = g_r3[rd, 0]
+        for d in range(1, 4):
+            total = total + g_r3[rd, d]
+        g_full[rd, z] = total
+        for d in FAR:
+            send(g_full.at[rd, z], g_full.at[rd, z], gram.at[3], z_dev(d))
         along_b(1)
 
-        arrived(g_full.at[rd, pl.ds(0, 15)], gram.at[2])
+        arrived(g_full.at[rd, pl.ds(0, 7)], gram.at[3])
         elim_g[...] = g_full[rd].reshape(K, K)
         elim_x[...] = (
             lax.broadcasted_iota(jnp.int32, (K, K), 0) == lax.broadcasted_iota(jnp.int32, (K, K), 1)
         ).astype(F32)
-        eliminate(128, 0)
-        eliminate(96, 4)
+        eliminate(0)
+        eliminate(4)
 
         arrived(r1a.at[rd], cross.at[1])
         total_0 = part[7, 0]
@@ -257,7 +254,7 @@
             t1[rd, 4 * half : 4 * half + 4] = total_1
         each(1, 8, lambda d: send(
             t1.at[rd, d - 1], r2.at[rd, 1, d - 1], cross.at[4], a_dev(d)))
-        eliminate(64, 8)
+        eliminate(8)
         arrived(r2.at[rd, 0], cross.at[3])
         arrived(r2.at[rd, 1], cross.at[4])
         sum_0, sum_1 = t0[rd, b_at], t1[rd, 7]
@@ -267,7 +264,7 @@
         r3[rd, x, 0] = sum_0
         r3[rd, x, 1] = sum_1
         each(1, NX, lambda d: send(r3.at[rd, x], r3.at[rd, x], cross.at[5], x_dev(d)))
-        eliminate(32, 12)
+        eliminate(12)
         arrived(r3.at[rd, pl.ds(0, NX - 1)], cross.at[5])
         whole = r3[rd, 0]
         for d in range(1, NX):
@@ -321,14 +318,17 @@
         scratch_shapes=[
             vmem((2 * TOK, D // 2), BF16),
             vmem((K, 256), BF16),
-            vmem((K, D // 2), BF16),
+            vmem((2, 4, 32, K), BF16),
+            vmem((8, 2, 32, K), BF16),
+            vmem((8, 2, 4, 32, K), BF16),
             vmem((2, 4, 256, K), F32),
             vmem((2, 4, 256, K), F32),
             vmem((K, 2 * TOK), BF16),
-            vmem((2, 16, 8, K), F32),
-            vmem((2, 15, 8, K), F32),
-            vmem((2, 16, 8, K), F32),
-            vmem((2, 16, 8, K), F32),
+            vmem((2, 8, 16, K), F32),
+            vmem((2, 7, 16, K), F32),
+            vmem((2, 8, 16, K), F32),
+            vmem((2, 4, 16, K), F32),
+            vmem((2, 8, 16, K), F32),
             vmem((K, K), F32),
             vmem((K, K), F32),
             vmem((K, K), F32),
@@ -343,15 +343,15 @@
             vmem((8, 2, 8, 16, K), BF16),
             vmem((2, 2, 16, K), F32),
             vmem((2, 8, 16, K), F32),
-            pltpu.SemaphoreType.DMA((3,)),
+            pltpu.SemaphoreType.DMA((2,)),
             pltpu.SemaphoreType.DMA((5, 2)),
             pltpu.SemaphoreType.DMA((2, 4, 2)),
-            pltpu.SemaphoreType.DMA((2, 3, 2)),
+            pltpu.SemaphoreType.DMA((2, 4, 2)),
             pltpu.SemaphoreType.DMA((2, 6, 2)),
             pltpu.SemaphoreType.DMA((6, 2)),
         ],
         compiler_params=pltpu.CompilerParams(
-            collective_id=0, has_side_effects=True, vmem_limit_bytes=58 * 1024 * 1024
+            collective_id=0, has_side_effects=True, vmem_limit_bytes=52 * 1024 * 1024
         ),
         name="range_finder",
     )(activations, probe_matrix)

time: 116 us -> 110 us (0.948)
  the two profiles are of different devices: /device:TPU:16 before, /device:TPU:2 now
where the time goes in v4:
time: 110 us
  Pallas kernels  107 us (97%)
  local copies, waits for them, and re-layouts  2.18 us (2%)
    pallas_call x1, Pallas kernels, on_device(): pl.pallas_call(kernel, out_shape=(jax.ShapeDtypeStruct((8, K), F32), jax....  107 us

profile of v4, /device:TPU:2, one launch (start us, length us, event | category | flops | bytes accessed | tf_op | source)
XLA Modules:
  0.0 110.0 jit_solution(7229511028449677660)
XLA Ops:
  0.6 0.0 copy-start
  0.6 0.8 copy-done
  1.5 107.2 %range_finder.1 = (f32[8,128]{1,0:T(8,128)S(1)}, f32[256,128]{1,0:T(8,128)S(1)}) custom-call(bf16[512,4096]{1,0:T(8,128)(2,1)} %act_hbm.1, bf16[128,256]{1,0:T(8,128)(2,1)S(1)} %copy-done), custom_call_target="tpu_custom_call" | custom-call | tf_op jit(solution)/shard_map/range_finder/pallas_call | solution.py:307
  108.7 0.8 copy.4
  109.4 0.6 copy.6
Async XLA Ops:
  0.6 0.8 copy-start

commit v5 on v4

--- a/solution.py
+++ b/solution.py
@@ -28,7 +28,7 @@
     act, p_in, p_own, p_line, p_full, half_out, half_in, sk,
     g_loc, g_r1, g_r2, g_r3, g_full, elim_g, elim_x, linv,
     part, s1, r1a, r1b, t0, t1, r2, r3,
-    bt, first, second,
+    bt, gathered, solved, first,
     in_sem, probe_sem, half_sem, gram_sem, cross_sem, gather_sem,
 ):
     grp, row = lax.axis_index("grp"), lax.axis_index("row")
@@ -114,13 +114,13 @@
 
     def both_halves(rd, product):
         def partial(q):
-            half_out[rd, q] = product(act[columns(q * 256, 256), :])
+            half_out[rd, q] = product(act[columns(q * TOK, TOK), :])
             send(half_out.at[rd, q], half_in.at[rd, q], half_sem.at[rd, q], sib)
 
-        each(0, 4, partial)
-        for q in range(4):
+        each(0, 2, partial)
+        for q in range(2):
             arrived(half_in.at[rd, q], half_sem.at[rd, q])
-            sk[:, q * 256 : q * 256 + 256] = (half_out[rd, q] + half_in[rd, q]).T.astype(BF16)
+            sk[:, q * TOK : q * TOK + TOK] = (half_out[rd, q] + half_in[rd, q]).T.astype(BF16)
 
     both_halves(0, lambda rows: jnp.dot(
         rows, p_full[...].reshape(2048, K), preferred_element_type=F32))
@@ -222,6 +222,7 @@
         along_b(0)
         each(7, 8, cross_to)
         cross_of(8)
+        along_b(1)
         arrived(g_r3.at[rd, pl.ds(0, 3)], gram.at[2])
         total = g_r3[rd, 0]
         for d in range(1, 4):
@@ -229,15 +230,6 @@
         g_full[rd, z] = total
         for d in FAR:
             send(g_full.at[rd, z], g_full.at[rd, z], gram.at[3], z_dev(d))
-        along_b(1)
-
-        arrived(g_full.at[rd, pl.ds(0, 7)], gram.at[3])
-        elim_g[...] = g_full[rd].reshape(K, K)
-        elim_x[...] = (
-            lax.broadcasted_iota(jnp.int32, (K, K), 0) == lax.broadcasted_iota(jnp.int32, (K, K), 1)
-        ).astype(F32)
-        eliminate(0)
-        eliminate(4)
 
         arrived(r1a.at[rd], cross.at[1])
         total_0 = part[7, 0]
@@ -254,7 +246,13 @@
             t1[rd, 4 * half : 4 * half + 4] = total_1
         each(1, 8, lambda d: send(
             t1.at[rd, d - 1], r2.at[rd, 1, d - 1], cross.at[4], a_dev(d)))
-        eliminate(8)
+        arrived(g_full.at[rd, pl.ds(0, 7)], gram.at[3])
+        elim_g[...] = g_full[rd].reshape(K, K)
+        elim_x[...] = (
+            lax.broadcasted_iota(jnp.int32, (K, K), 0) == lax.broadcasted_iota(jnp.int32, (K, K), 1)
+        ).astype(F32)
+        eliminate(0)
+        eliminate(4)
         arrived(r2.at[rd, 0], cross.at[3])
         arrived(r2.at[rd, 1], cross.at[4])
         sum_0, sum_1 = t0[rd, b_at], t1[rd, 7]
@@ -263,41 +261,54 @@
             sum_1 = sum_1 + r2[rd, 1, d]
         r3[rd, x, 0] = sum_0
         r3[rd, x, 1] = sum_1
-        each(1, NX, lambda d: send(r3.at[rd, x], r3.at[rd, x], cross.at[5], x_dev(d)))
-        eliminate(12)
+        for d in (2, 1, 3):
+            send(r3.at[rd, x], r3.at[rd, x], cross.at[5], x_dev(d))
+        eliminate(8)
         arrived(r3.at[rd, pl.ds(0, NX - 1)], cross.at[5])
         whole = r3[rd, 0]
         for d in range(1, NX):
             whole = whole + r3[rd, d]
-        solved = lax.dot_general(
-            whole.reshape(32, K), linv[...], NT, precision=lax.Precision.HIGHEST,
+        return whole
+
+    def finish(wide):
+        return lax.dot_general(
+            wide[...].reshape(256, K), linv[...], NT, precision=lax.Precision.HIGHEST,
             preferred_element_type=F32,
-        )
-        return solved.reshape(2, 16, K)
-
-    solved = solve_round(0, y, z, y_dev, z_dev)
-    first[c] = solved
-    for h in range(2):
-        bt[y, h, z] = solved[h].astype(BF16)
-    each(1, NZ, lambda d: send(bt.at[y, 0, z], bt.at[y, 0, z], gather_sem.at[0], z_dev(d)))
-    each(1, NY, lambda d: send(bt.at[y, 1, z], bt.at[y, 1, z], gather_sem.at[1], y_dev(d)))
-    arrived(bt.at[0, 0, pl.ds(0, 7)], gather_sem.at[0])
-    each(1, NY, lambda d: send(bt.at[y, 0], bt.at[y, 0], gather_sem.at[2], y_dev(d)))
-    arrived(bt.at[pl.ds(0, 7), 0, 0], gather_sem.at[1])
-    each(1, NZ, lambda d: send(bt.at[:, 1, z], bt.at[:, 1, z], gather_sem.at[3], z_dev(d)))
+        ).reshape(2, 8, 16, K)
+
+    whole = solve_round(0, y, z, y_dev, z_dev)
+    wide = gathered.at[0]
+    wide[0, z] = whole[0]
+    wide[1, y] = whole[1]
+    for d in FAR:
+        send(wide.at[0, z], wide.at[0, z], gather_sem.at[0], z_dev(d))
+        send(wide.at[1, y], wide.at[1, y], gather_sem.at[1], y_dev(d))
+    eliminate(12)
+    arrived(wide.at[0, pl.ds(0, 7)], gather_sem.at[0])
+    arrived(wide.at[1, pl.ds(0, 7)], gather_sem.at[1])
+    solved[...] = finish(wide)
+    bt[y, 0] = solved[0].astype(BF16)
+    bt[:, 1, z] = solved[1].astype(BF16)
+    for d in FAR:
+        send(bt.at[y, 0], bt.at[y, 0], gather_sem.at[2], y_dev(d))
+        send(bt.at[:, 1, z], bt.at[:, 1, z], gather_sem.at[3], z_dev(d))
+    first[c, 0] = solved[0, z]
+    first[c, 1] = solved[1, y]
     send(first.at[c], first.at[c], gather_sem.at[4], sib)
     arrived(bt.at[pl.ds(0, 7), 0], gather_sem.at[2])
     arrived(bt.at[:, 0, pl.ds(0, 7)], gather_sem.at[3])
     both_halves(1, lambda rows: jnp.dot(
         rows, bt[...].reshape(2048, K), preferred_element_type=F32))
 
-    solved = solve_round(1, z, y, z_dev, y_dev)
-    second[:, y] = solved
-    each(1, NY, lambda d: send(second.at[:, y], second.at[:, y], gather_sem.at[5], y_dev(d)))
+    wide = gathered.at[1]
+    wide[:, y] = solve_round(1, z, y, z_dev, y_dev)
+    for d in FAR:
+        send(wide.at[:, y], wide.at[:, y], gather_sem.at[5], y_dev(d))
+    eliminate(12)
     arrived(first.at[0], gather_sem.at[4])
     out_first[...] = first[lax.div(x, 2), lax.rem(x, 2), pl.ds(pl.multiple_of(8 * c, 8), 8), :]
-    arrived(second.at[:, pl.ds(0, 7)], gather_sem.at[5])
-    out_second[...] = second[...].reshape(256, K)
+    arrived(wide.at[:, pl.ds(0, 7)], gather_sem.at[5])
+    out_second[...] = finish(wide).reshape(256, K)
     for ref, sems in sent:
         pltpu.make_async_copy(ref, ref, sems.at[0]).wait()
 
@@ -321,8 +332,8 @@
             vmem((2, 4, 32, K), BF16),
             vmem((8, 2, 32, K), BF16),
             vmem((8, 2, 4, 32, K), BF16),
-            vmem((2, 4, 256, K), F32),
-            vmem((2, 4, 256, K), F32),
+            vmem((2, 2, TOK, K), F32),
+            vmem((2, 2, TOK, K), F32),
             vmem((K, 2 * TOK), BF16),
             vmem((2, 8, 16, K), F32),
             vmem((2, 7, 16, K), F32),
@@ -341,11 +352,12 @@
             vmem((2, 2, 7, 16, K), F32),
             vmem((2, NX, 2, 16, K), F32),
             vmem((8, 2, 8, 16, K), BF16),
+            vmem((2, 2, 8, 16, K), F32),
+            vmem((2, 8, 16, K), F32),
             vmem((2, 2, 16, K), F32),
-            vmem((2, 8, 16, K), F32),
             pltpu.SemaphoreType.DMA((2,)),
             pltpu.SemaphoreType.DMA((5, 2)),
-            pltpu.SemaphoreType.DMA((2, 4, 2)),
+            pltpu.SemaphoreType.DMA((2, 2, 2)),
             pltpu.SemaphoreType.DMA((2, 4, 2)),
             pltpu.SemaphoreType.DMA((2, 6, 2)),
             pltpu.SemaphoreType.DMA((6, 2)),

time: 110 us -> 107 us (0.973)
  Pallas kernels: 107 us -> 104 us
    pallas_call x1, Pallas kernels: 107 us -> 104 us  [on_device(): pl.pallas_call(kernel, out_shape=(jax.ShapeDtypeStruct((8, K), F32), jax....]
where the time goes in v5:
time: 107 us; the launch traced here: 106 us
  Pallas kernels  104 us (97%)
  local copies, waits for them, and re-layouts  2.18 us (2%)
    pallas_call x1, Pallas kernels, on_device(): pl.pallas_call(kernel, out_shape=(jax.ShapeDtypeStruct((8, K), F32), jax....  104 us
    unnamed x4, local copies, waits for them, and re-layouts  2.18 us

profile of v5, /device:TPU:2, one launch (start us, length us, event | category | flops | bytes accessed | tf_op | source)
XLA Modules:
  0.0 106.4 jit_solution(6029241321191697230)
XLA Ops:
  0.6 0.0 copy-start
  0.6 0.8 copy-done
  1.5 103.5 %range_finder.1 = (f32[8,128]{1,0:T(8,128)S(1)}, f32[256,128]{1,0:T(8,128)S(1)}) custom-call(bf16[512,4096]{1,0:T(8,128)(2,1)} %act_hbm.1, bf16[128,256]{1,0:T(8,128)(2,1)S(1)} %copy-done), custom_call_target="tpu_custom_call" | custom-call | tf_op jit(solution)/shard_map/range_finder/pallas_call | solution.py:318
  105.0 0.8 copy.4
  105.8 0.6 copy.6
Async XLA Ops:
  0.6 0.8 copy-start

commit v6 on v5

--- a/solution.py
+++ b/solution.py
@@ -27,9 +27,9 @@
     act_hbm, probe_hbm, out_first, out_second,
     act, p_in, p_own, p_line, p_full, half_out, half_in, sk,
     g_loc, g_r1, g_r2, g_r3, g_full, elim_g, elim_x, linv,
-    part, s1, r1a, r1b, t0, t1, r2, r3,
+    part_a, part_b, s1a, s1b, s2b, ra, rb, r1a, r1b, t0, t1, r2, r3,
     bt, gathered, solved, first,
-    in_sem, probe_sem, half_sem, gram_sem, cross_sem, gather_sem,
+    in_sem, probe_sem, half_sem, gram_sem, cross_sem, far_sem, gather_sem, line_sem,
 ):
     grp, row = lax.axis_index("grp"), lax.axis_index("row")
     y, x = lax.div(grp, NX), lax.rem(grp, NX)
@@ -187,23 +187,51 @@
         for d in FAR:
             send(g_loc.at[rd, lax.rem(z + d, 8)], g_r1.at[rd, d - 1], gram.at[0], z_dev(d))
 
-        def cross_of(d):
+        turn = 2 + 4 * c
+
+        def cross_of(d, at):
             a = lax.rem(a_at + d, 8)
             term = jnp.dot(sk[...], act[:, columns(a * 256, 256)], preferred_element_type=F32)
             term = term.T.reshape(2, 8, 16, K)
-            part[d - 1] = term
-            s1[rd, d - 1] = term.astype(BF16)
-
-        def cross_to(d):
-            cross_of(d)
-            send(s1.at[rd, d - 1, 0], r1a.at[rd, d - 1], cross.at[1], a_dev(d))
-
-        def along_b(half):
-            each(1, 8, lambda d: send(
-                s1.at[rd, pl.ds(4 * half, 4), 1, lax.rem(b_at + d, 8)],
-                r1b.at[rd, half, d - 1], cross.at[2 * half], b_dev(d)))
-
-        each(1, 5, cross_to)
+            part_b[at] = term[1]
+            s1b[rd, at] = term[1].astype(BF16)
+            return term[0]
+
+        def far(k):
+            slot = lax.rem(k + 2, 3)
+            s1a[rd, k] = cross_of(4 - k + 3 * lax.div(k, 2), k).astype(BF16)
+            send(s1a.at[rd, k], ra.at[rd, slot], cross.at[6], a_dev(jnp.where(k == 0, turn, 6 * k - 5)))
+
+        def near(k):
+            s1a[rd, 3 + k] = cross_of(1 + 6 * k, 3 + k).astype(BF16)
+            send(s1a.at[rd, 3 + k], r1a.at[rd, k], cross.at[1], a_dev(1 + 6 * k))
+
+        def middle(k):
+            term = cross_of(2 + 4 * k, 5 + k)
+            shared = ra[rd, 2].astype(F32) * (k == c).astype(F32)
+            s1a[rd, 5 + k] = (term + ra[rd, k].astype(F32) + shared).astype(BF16)
+            send(s1a.at[rd, 5 + k], r1a.at[rd, 2 + k], cross.at[1], a_dev(2 + 4 * k))
+
+        def b_block(half, e):
+            return s1b.at[rd, pl.ds(4 * half, 4), lax.rem(b_at + e, 8)]
+
+        def start_b(half):
+            send(b_block(half, 4), rb.at[rd, half, 2], far_sem.at[rd, half], b_dev(turn))
+            send(b_block(half, 3), rb.at[rd, half, 0], far_sem.at[rd, half], b_dev(1))
+            send(b_block(half, 5), rb.at[rd, half, 1], far_sem.at[rd, half], b_dev(7))
+            for k in range(2):
+                send(b_block(half, 1 + 6 * k), r1b.at[rd, half, k], cross.at[2 * half], b_dev(1 + 6 * k))
+
+        def end_b(half):
+            arrived(rb.at[rd, half], far_sem.at[rd, half])
+            for k in range(2):
+                term = part_b[4 * half : 4 * half + 4, lax.rem(b_at + 2 + 4 * k, 8)]
+                shared = rb[rd, half, 2].astype(F32) * (k == c).astype(F32)
+                s2b[rd, half, k] = (term + rb[rd, half, k].astype(F32) + shared).astype(BF16)
+                send(s2b.at[rd, half, k], r1b.at[rd, half, 2 + k], cross.at[2 * half], b_dev(2 + 4 * k))
+
+        each(0, 3, far)
+        each(0, 2, near)
         arrived(g_r1.at[rd], gram.at[0])
         total = g_loc[rd, z]
         for d in range(7):
@@ -211,7 +239,9 @@
         g_r2[rd, y] = total
         for d in FAR:
             send(g_r2.at[rd, y], g_r2.at[rd, y], gram.at[1], y_dev(d))
-        each(5, 7, cross_to)
+        start_b(0)
+        arrived(ra.at[rd], cross.at[6])
+        each(0, 2, middle)
         arrived(g_r2.at[rd, pl.ds(0, 7)], gram.at[1])
         total = g_r2[rd, 0]
         for d in range(1, 8):
@@ -219,10 +249,9 @@
         g_r3[rd, x] = total
         for d in (2, 1, 3):
             send(g_r3.at[rd, x], g_r3.at[rd, x], gram.at[2], x_dev(d))
-        along_b(0)
-        each(7, 8, cross_to)
-        cross_of(8)
-        along_b(1)
+        part_a[...] = cross_of(0, 7)
+        start_b(1)
+        end_b(0)
         arrived(g_r3.at[rd, pl.ds(0, 3)], gram.at[2])
         total = g_r3[rd, 0]
         for d in range(1, 4):
@@ -230,28 +259,29 @@
         g_full[rd, z] = total
         for d in FAR:
             send(g_full.at[rd, z], g_full.at[rd, z], gram.at[3], z_dev(d))
+        end_b(1)
 
         arrived(r1a.at[rd], cross.at[1])
-        total_0 = part[7, 0]
-        for d in range(7):
+        total_0 = part_a[...]
+        for d in range(4):
             total_0 = total_0 + r1a[rd, d].astype(F32)
         t0[rd] = total_0
         each(1, 8, lambda d: send(
             t0.at[rd, lax.rem(b_at + d, 8)], r2.at[rd, 0, d - 1], cross.at[3], b_dev(d)))
-        for half in range(2):
-            arrived(r1b.at[rd, half], cross.at[2 * half])
-            total_1 = part[4 * half : 4 * half + 4, 1, b_at]
-            for d in range(7):
-                total_1 = total_1 + r1b[rd, half, d].astype(F32)
-            t1[rd, 4 * half : 4 * half + 4] = total_1
-        each(1, 8, lambda d: send(
-            t1.at[rd, d - 1], r2.at[rd, 1, d - 1], cross.at[4], a_dev(d)))
         arrived(g_full.at[rd, pl.ds(0, 7)], gram.at[3])
         elim_g[...] = g_full[rd].reshape(K, K)
         elim_x[...] = (
             lax.broadcasted_iota(jnp.int32, (K, K), 0) == lax.broadcasted_iota(jnp.int32, (K, K), 1)
         ).astype(F32)
         eliminate(0)
+        for half in range(2):
+            arrived(r1b.at[rd, half], cross.at[2 * half])
+            total_1 = part_b[4 * half : 4 * half + 4, b_at]
+            for d in range(4):
+                total_1 = total_1 + r1b[rd, half, d].astype(F32)
+            t1[rd, 4 * half : 4 * half + 4] = total_1
+        for at, d in enumerate((4, 3, 5, 1, 7, 2, 6)):
+            send(t1.at[rd, at], r2.at[rd, 1, at], cross.at[4], a_dev(d))
         eliminate(4)
         arrived(r2.at[rd, 0], cross.at[3])
         arrived(r2.at[rd, 1], cross.at[4])
@@ -289,14 +319,30 @@
     solved[...] = finish(wide)
     bt[y, 0] = solved[0].astype(BF16)
     bt[:, 1, z] = solved[1].astype(BF16)
-    for d in FAR:
-        send(bt.at[y, 0], bt.at[y, 0], gather_sem.at[2], y_dev(d))
-        send(bt.at[:, 1, z], bt.at[:, 1, z], gather_sem.at[3], z_dev(d))
+    def of_y(d):
+        return bt.at[lax.rem(y + d, 8), 0]
+
+    def of_z(d):
+        return bt.at[:, 1, lax.rem(z + d, 8)]
+
+    axes = ((of_y, y_dev, line_sem.at[0]), (of_z, z_dev, line_sem.at[1]))
+    for k, d in ((1, 2), (2, 6), (0, 1), (0, 7)):
+        for block, dev, sems in axes:
+            send(block(0), block(0), sems.at[k], dev(d))
     first[c, 0] = solved[0, z]
     first[c, 1] = solved[1, y]
     send(first.at[c], first.at[c], gather_sem.at[4], sib)
-    arrived(bt.at[pl.ds(0, 7), 0], gather_sem.at[2])
-    arrived(bt.at[:, 0, pl.ds(0, 7)], gather_sem.at[3])
+    piece = bt.at[0, 0]
+    for k, d in ((1, 6), (2, 2)):
+        for block, dev, sems in axes:
+            arrived(piece, sems.at[k])
+            send(block(d), block(d), sems.at[3], dev(1 if d == 6 else 7))
+    turned = 6 - 4 * c
+    for block, dev, sems in axes:
+        send(block(turned), block(turned), sems.at[3], dev(2 + 4 * c))
+    for block, dev, sems in axes:
+        arrived(bt.at[pl.ds(0, 2), 0], sems.at[0])
+        arrived(bt.at[pl.ds(0, 3), 0], sems.at[3])
     both_halves(1, lambda rows: jnp.dot(
         rows, bt[...].reshape(2048, K), preferred_element_type=F32))
 
@@ -343,10 +389,15 @@
             vmem((K, K), F32),
             vmem((K, K), F32),
             vmem((K, K), F32),
-            vmem((8, 2, 8, 16, K), F32),
-            vmem((2, 8, 2, 8, 16, K), BF16),
+            vmem((8, 16, K), F32),
+            vmem((8, 8, 16, K), F32),
             vmem((2, 7, 8, 16, K), BF16),
-            vmem((2, 2, 7, 4, 16, K), BF16),
+            vmem((2, 8, 8, 16, K), BF16),
+            vmem((2, 2, 2, 4, 16, K), BF16),
+            vmem((2, 3, 8, 16, K), BF16),
+            vmem((2, 2, 3, 4, 16, K), BF16),
+            vmem((2, 4, 8, 16, K), BF16),
+            vmem((2, 2, 4, 4, 16, K), BF16),
             vmem((2, 8, 16, K), F32),
             vmem((2, 8, 16, K), F32),
             vmem((2, 2, 7, 16, K), F32),
@@ -359,8 +410,10 @@
             pltpu.SemaphoreType.DMA((5, 2)),
             pltpu.SemaphoreType.DMA((2, 2, 2)),
             pltpu.SemaphoreType.DMA((2, 4, 2)),
-            pltpu.SemaphoreType.DMA((2, 6, 2)),
+            pltpu.SemaphoreType.DMA((2, 7, 2)),
+            pltpu.SemaphoreType.DMA((2, 2, 2)),
             pltpu.SemaphoreType.DMA((6, 2)),
+            pltpu.SemaphoreType.DMA((2, 4, 2)),
         ],
         compiler_params=pltpu.CompilerParams(
             collective_id=0, has_side_effects=True, vmem_limit_bytes=52 * 1024 * 1024

time: 107 us -> 105 us (0.981)
  the two profiles are of different devices: /device:TPU:2 before, /device:TPU:8 now
where the time goes in v6:
time: 105 us
  Pallas kernels  102 us (97%)
  local copies, waits for them, and re-layouts  2.18 us (2%)
    pallas_call x1, Pallas kernels, on_device(): pl.pallas_call(kernel, out_shape=(jax.ShapeDtypeStruct((8, K), F32), jax....  102 us
    unnamed x4, local copies, waits for them, and re-layouts  2.18 us

profile of v6, /device:TPU:8, one launch (start us, length us, event | category | flops | bytes accessed | tf_op | source)
XLA Modules:
  0.0 104.9 jit_solution(16785504311062611093)
XLA Ops:
  0.6 0.0 copy-start
  0.6 0.8 copy-done
  1.5 102.0 %range_finder.1 = (f32[8,128]{1,0:T(8,128)S(1)}, f32[256,128]{1,0:T(8,128)S(1)}) custom-call(bf16[512,4096]{1,0:T(8,128)(2,1)} %act_hbm.1, bf16[128,256]{1,0:T(8,128)(2,1)S(1)} %copy-done), custom_call_target="tpu_custom_call" | custom-call | tf_op jit(solution)/shard_map/range_finder/pallas_call | solution.py:364
  103.5 0.8 copy.4
  104.3 0.6 copy.6
Async XLA Ops:
  0.6 0.8 copy-start

commit v7 on v5

--- a/solution.py
+++ b/solution.py
@@ -211,7 +211,8 @@
         g_r2[rd, y] = total
         for d in FAR:
             send(g_r2.at[rd, y], g_r2.at[rd, y], gram.at[1], y_dev(d))
-        each(5, 7, cross_to)
+        along_b(0)
+        each(5, 8, cross_to)
         arrived(g_r2.at[rd, pl.ds(0, 7)], gram.at[1])
         total = g_r2[rd, 0]
         for d in range(1, 8):
@@ -219,8 +220,6 @@
         g_r3[rd, x] = total
         for d in (2, 1, 3):
             send(g_r3.at[rd, x], g_r3.at[rd, x], gram.at[2], x_dev(d))
-        along_b(0)
-        each(7, 8, cross_to)
         cross_of(8)
         along_b(1)
         arrived(g_r3.at[rd, pl.ds(0, 3)], gram.at[2])
@@ -238,6 +237,12 @@
         t0[rd] = total_0
         each(1, 8, lambda d: send(
             t0.at[rd, lax.rem(b_at + d, 8)], r2.at[rd, 0, d - 1], cross.at[3], b_dev(d)))
+        arrived(g_full.at[rd, pl.ds(0, 7)], gram.at[3])
+        elim_g[...] = g_full[rd].reshape(K, K)
+        elim_x[...] = (
+            lax.broadcasted_iota(jnp.int32, (K, K), 0) == lax.broadcasted_iota(jnp.int32, (K, K), 1)
+        ).astype(F32)
+        eliminate(0)
         for half in range(2):
             arrived(r1b.at[rd, half], cross.at[2 * half])
             total_1 = part[4 * half : 4 * half + 4, 1, b_at]
@@ -246,12 +251,6 @@
             t1[rd, 4 * half : 4 * half + 4] = total_1
         each(1, 8, lambda d: send(
             t1.at[rd, d - 1], r2.at[rd, 1, d - 1], cross.at[4], a_dev(d)))
-        arrived(g_full.at[rd, pl.ds(0, 7)], gram.at[3])
-        elim_g[...] = g_full[rd].reshape(K, K)
-        elim_x[...] = (
-            lax.broadcasted_iota(jnp.int32, (K, K), 0) == lax.broadcasted_iota(jnp.int32, (K, K), 1)
-        ).astype(F32)
-        eliminate(0)
         eliminate(4)
         arrived(r2.at[rd, 0], cross.at[3])
         arrived(r2.at[rd, 1], cross.at[4])

time: 107 us -> 104 us (0.972)
  Pallas kernels: 104 us -> 101 us
    pallas_call x1, Pallas kernels: 104 us -> 101 us  [on_device(): pl.pallas_call(kernel, out_shape=(jax.ShapeDtypeStruct((8, K), F32), jax....]
where the time goes in v7:
time: 104 us
  Pallas kernels  101 us (97%)
  local copies, waits for them, and re-layouts  2.18 us (2%)
    pallas_call x1, Pallas kernels, on_device(): pl.pallas_call(kernel, out_shape=(jax.ShapeDtypeStruct((8, K), F32), jax....  101 us
    unnamed x4, local copies, waits for them, and re-layouts  2.18 us

profile of v7, /device:TPU:2, one launch (start us, length us, event | category | flops | bytes accessed | tf_op | source)
XLA Modules:
  0.0 104.1 jit_solution(1405815388025090653)
XLA Ops:
  0.6 0.0 copy-start
  0.6 0.8 copy-done
  1.5 101.3 %range_finder.1 = (f32[8,128]{1,0:T(8,128)S(1)}, f32[256,128]{1,0:T(8,128)S(1)}) custom-call(bf16[512,4096]{1,0:T(8,128)(2,1)} %act_hbm.1, bf16[128,256]{1,0:T(8,128)(2,1)S(1)} %copy-done), custom_call_target="tpu_custom_call" | custom-call | tf_op jit(solution)/shard_map/range_finder/pallas_call | solution.py:317
  102.8 0.8 copy.4
  103.5 0.6 copy.6
Async XLA Ops:
  0.6 0.8 copy-start
